TPU v7x, 256 devices: a whole 4x4x8 slice. The times are simulated.
256 devices in a mesh: dp: 16 (over z, core), ctx: 16 (over x, y).
Axes of the slice: x: 4, y: 4, z: 8, core: 2. Of those that a mesh axis runs over, the one named last changes fastest.
Arguments:
- ssm_input: bfloat16 [16, 4096, 5120], P('dp', 'ctx'), may hold values from -6 to 6
- gate_input: bfloat16 [16, 4096, 5120], P('dp', 'ctx'), may hold values from -6 to 6
- input_map: bfloat16 [16, 4096, 128], P('dp', 'ctx'), may hold values from -6 to 6
- output_map: bfloat16 [16, 4096, 128], P('dp', 'ctx'), may hold values from -6 to 6
- step_size: float32 [16, 80, 4096], P('dp', None, 'ctx'), may hold values from 0.00024414062 to 1.2009766
- log_rate: float32 [80], replicated
- entry_state: bfloat16 [16, 16, 80, 64, 128], P('dp', 'ctx'), may hold values from -0.59765625 to 0.59765625
- norm_gain: float32 [5120], replicated, may hold values from 0.18 to 5.5
- out_weight: bfloat16 [5120, 1280], P(('dp', 'ctx')), may hold values from -0.078125 to 0.078125
- out_grad: bfloat16 [16, 4096, 1280], P('dp', 'ctx')
Outputs:
- input_grad: bfloat16 [16, 4096, 5120], P('dp', 'ctx')
- clipped_grad: float32 [5120, 1280], P('ctx', 'dp')
All inputs are finite; a program needn't handle non-finite values.
Results may differ from a plain program's by a relative error of at most 0.014.
Values may be sent and summed in bfloat16 or wider, within the bound.
A program may use at most 192 MiB of HBM per device.

v0:
```python
import math

import jax
import jax.numpy as jnp
from jax import lax
from jax.sharding import PartitionSpec as P

NORM_EPS = 1e-05
CLIP_EPS = 1e-06


def carried_in(value, axis, combine, identity):
    length, position = (lax.axis_size(axis), lax.axis_index(axis))
    everything = jax.tree.map(lambda part: lax.all_gather(part, axis), value)
    start = jax.tree.map(
        lambda part, zero: jnp.broadcast_to(jnp.asarray(zero, part.dtype), part.shape),
        value,
        identity,
    )

    def turn(k, before):
        at = length - 1 - k
        reached = at > position
        new = combine(before, jax.tree.map(lambda part: part[at], everything))
        return jax.tree.map(lambda a, b: jnp.where(reached, a, b), new, before)

    return lax.fori_loop(0, length, turn, start)


def head_block(scaled, cumulative, coupling, c_full, b_full, start_state):
    length = cumulative.shape[-1]
    log_gap = cumulative[:, :, :, None] - cumulative[:, :, None, :]
    causal = jnp.arange(length)[:, None] >= jnp.arange(length)[None, :]
    decay_map = jnp.exp(jnp.where(causal, log_gap, -1e30))
    mixing = decay_map * coupling[:, None, :, :]
    inside = jnp.einsum("egtu,eugp->etgp", mixing, scaled)
    carried = jnp.einsum("etn,egpn->etgp", c_full, start_state)
    carried = carried * jnp.exp(cumulative).transpose(0, 2, 1)[:, :, :, None]
    final_log = cumulative[:, :, -1:]
    tail_decay = jnp.exp(final_log - cumulative)
    end_state = jnp.exp(final_log)[:, :, :, None] * start_state
    end_state = end_state + jnp.einsum("egu,eugp,eun->egpn", tail_decay, scaled, b_full)
    return (inside + carried, end_state)


def scan_forward(values, step, rate_vec, b_full, c_full, start_state):
    blocks, length, inner_dim = values.shape
    head_count = rate_vec.shape[0]
    head_size = inner_dim // head_count
    group_size = math.gcd(head_count, 8)
    group_count = head_count // group_size
    cumulative = jnp.cumsum(-step * rate_vec[None, :, None], axis=-1)
    scaled = (
        values.reshape(blocks, length, head_count, head_size)
        * step.transpose(0, 2, 1)[:, :, :, None]
    )
    coupling = jnp.einsum("etn,eun->etu", c_full, b_full)
    scaled_groups = scaled.reshape(blocks, length, group_count, group_size, head_size).transpose(
        2, 0, 1, 3, 4
    )
    cumul_groups = cumulative.reshape(blocks, group_count, group_size, length).transpose(1, 0, 2, 3)
    state_groups = start_state.reshape(blocks, group_count, group_size, head_size, -1).transpose(
        1, 0, 2, 3, 4
    )

    def per_block(operands):
        return head_block(operands[0], operands[1], coupling, c_full, b_full, operands[2])

    outputs, finals = lax.map(per_block, (scaled_groups, cumul_groups, state_groups))
    y_value = outputs.transpose(1, 2, 0, 3, 4).reshape(blocks, length, inner_dim)
    end_state = finals.transpose(1, 0, 2, 3, 4).reshape(blocks, head_count, head_size, -1)
    return (y_value, end_state)


def gated_norm(values, gate_f, norm_gain):
    mixed = values * jax.nn.silu(gate_f)
    inverse_rms = lax.rsqrt(jnp.mean(mixed * mixed, axis=-1, keepdims=True) + NORM_EPS)
    return mixed * inverse_rms * norm_gain


def chain_terms(y_grad, step, rate_vec, c_full):
    blocks, length, inner_dim = y_grad.shape
    head_count = rate_vec.shape[0]
    cumulative = jnp.cumsum(-step * rate_vec[None, :, None], axis=-1)
    weighted = (
        y_grad.reshape(blocks, length, head_count, -1)
        * jnp.exp(cumulative).transpose(0, 2, 1)[:, :, :, None]
    )
    pushed = jnp.einsum("ethp,etn->ehpn", weighted, c_full)
    return (jnp.exp(cumulative[:, :, -1]), pushed)


def combine_maps(first_part, second_part):
    return (
        first_part[0] * second_part[0],
        second_part[0][:, :, None, None] * first_part[1] + second_part[1],
    )


def per_device(
    ssm_input,
    gate_input,
    input_map,
    output_map,
    step_size,
    log_rate,
    entry_state,
    norm_gain,
    out_weight,
    out_grad,
):
    examples, length, inner_dim = ssm_input.shape
    model_dim = out_grad.shape[-1]
    head_count = log_rate.shape[0]
    rate_vec = jnp.exp(log_rate)
    flat_grad = out_grad.reshape(examples * length, model_dim)
    gated_grad_all = lax.dot_general(
        flat_grad,
        lax.all_gather(out_weight, ("dp", "ctx"), axis=0, tiled=True),
        (((1,), (1,)), ((), ())),
        preferred_element_type=jnp.float32,
    ).reshape(examples, length, inner_dim)
    values = ssm_input.astype(jnp.float32)
    b_full = input_map.astype(jnp.float32)
    c_full = output_map.astype(jnp.float32)
    gate_f = gate_input.astype(jnp.float32)
    start_state = entry_state.reshape(examples, head_count, -1, b_full.shape[-1]).astype(
        jnp.float32
    )

    def forward(inputs_f):
        return scan_forward(inputs_f, step_size, rate_vec, b_full, c_full, start_state)

    (y_value, end_state), pullback = jax.vjp(forward, values)

    def normalize(inputs_y):
        return gated_norm(inputs_y, gate_f, norm_gain)

    normed, norm_pull = jax.vjp(normalize, y_value)
    gated = normed.astype(jnp.bfloat16)
    (y_grad,) = norm_pull(gated_grad_all)
    factors, pushed = chain_terms(y_grad, step_size, rate_vec, c_full)
    identity = (jnp.ones_like(factors), jnp.zeros_like(pushed))
    _, state_grad = carried_in((factors, pushed), "ctx", combine_maps, identity)
    (input_f,) = pullback((y_grad, state_grad))
    input_grad = input_f.astype(jnp.bfloat16)
    columns = lax.all_to_all(gated, "ctx", split_axis=2, concat_axis=1, tiled=True)
    term = jnp.einsum(
        "eti,etd->eid",
        columns,
        lax.all_gather(out_grad, "ctx", axis=1, tiled=True),
        preferred_element_type=jnp.float32,
    )
    squares = jnp.sum(term * term, axis=(1, 2))
    total_sq = lax.psum(squares, "ctx")
    clip = jnp.minimum(1.0, lax.rsqrt(total_sq + CLIP_EPS))
    clipped = jnp.sum(clip[:, None, None] * term, axis=0)
    scale = math.sqrt(inner_dim * model_dim / (examples * lax.axis_size("dp")))
    summed = lax.psum_scatter(clipped, "dp", scatter_dimension=1, tiled=True)
    return (input_grad, summed * scale)


def solution(mesh):
    placed = (
        P("dp", "ctx", None),
        P("dp", "ctx", None),
        P("dp", "ctx", None),
        P("dp", "ctx", None),
        P("dp", None, "ctx"),
        P(),
        P("dp", "ctx", None, None, None),
        P(),
        P(("dp", "ctx"), None),
        P("dp", "ctx", None),
    )
    return jax.shard_map(
        per_device,
        mesh=mesh,
        in_specs=placed,
        out_specs=(P("dp", "ctx", None), P("ctx", "dp")),
        check_vma=False,
    )
```

profile of v0, /device:TPU:7, one launch (start us, length us, event | category | flops | bytes accessed | tf_op | source)
XLA Modules:
  0.0 706.6 jit_solution(8037400069180838587)
XLA Ops:
  11.4 4.9 copy.94
  16.5 4.8 multiply_bitcast_fusion
  21.5 2.9 broadcast.143.clone
  24.4 53.1 %while.48 = (s32[]{:T(128)}, f32[10,1,256,8,64]{2,4,3,1,0:T(8,128)}, bf16[10,1,8,256,256]{4,3,2,1,0:T(8,128)(2,1)}, f32[10,1,8,256]{3,2,1,0:T(8,128)S(1)}, bf16[...) while((s32[]{:T(128)}, ...), condition=%wide.region_3.4_spmd.clone.clone, body=%wide.region_2.3_spmd.clone.clone.sunk | while | flops 104073216 | bytes 4901557 | solution.py:69
  53.9 2.4 fusion.104
  77.5 5.9 copy.99
  83.4 55.9 %all-gather.11.cloned.1.call-done = bf16[256,20,1280]{2,1,0:T(8,128)(2,1)} async-done(((bf16[1,20,1280]{2,1,0:T(8,128)(2,1)}), bf16[256,20,1280]{2,1,0:T(8,128)(2,1)}) %all-gather.11.cloned.1.call-update) | async-done | bytes 13107216 | tf_op jit(solution)/shard_map/all_gather | solution.py:119
  139.3 19.8 %reshape.485 = bf16[5120,1280]{1,0:T(8,128)(2,1)} reshape(bf16[256,20,1280]{2,1,0:T(8,128)(2,1)} %all-gather.11.cloned.1.call-done) | data formatting | bytes 26214400
  159.2 14.6 %multiply_reduce_fusion = (f32[256]{0:T(256)S(1)}, f32[256]{0:T(256)S(1)}, f32[1,256,5120]{2,1,0:T(8,128)}, f32[256,5120]{1,0:T(8,128)}) fusion(f32[1,256,5120]{2,1,0:T(8,128)} %copy.99, bf16[1,256,5120]{2,1,0:T(8,128)(2,1)S(1)} %copy-done.1, f32[5120]{0:T(1024)S(1)} %copy-done.4, bf16[5120,1280]{1,0:T(8,128)(2,1)} %reshape.485, ...), kind=kOutput, calls=%fused_computation.69 | convolution fusion | flops 3369860608 | bytes 32135168 | tf_op jit(solution)/shard_map/dot_general | solution.py:117
  173.8 3.2 multiply_convert_fusion
  177.0 8.3 %copy.108 = bf16[1,256,5120]{1,0,2:T(2,128)(2,1)} copy(bf16[1,256,5120]{2,1,0:T(8,128)(2,1)S(1)} %multiply_convert_fusion) | data formatting | bytes 5242880 | tf_op jit(solution)/shard_map/convert_element_type | solution.py:140
  185.8 26.6 %reduce.8 = bf16[5120,256]{1,0:T(8,128)(2,1)S(1)} reduce(bf16[5120,1,256]{2,1,0:T(2,128)(2,1)} %bitcast.259, bf16[]{:T(256)} %broadcast.174), dimensions={1}, to_apply=%bitcast.197.reduce_sub_computation | reduce | bytes 5242882
  214.5 36.7 %all_to_all.15 = bf16[16,2,40960]{2,1,0:T(2,128)(2,1)S(1)} all-to-all(bf16[16,2,40960]{2,1,0:T(2,128)(2,1)} %reshape.498), channel_id=1, replica_groups=mesh['dp'=16,'ctx'=16] {'ctx'}, dimensions={0} | all-to-all | bytes 5242880 | tf_op jit(solution)/shard_map/all_to_all | solution.py:147
  251.2 7.2 %reshape.499 = bf16[5120,1,256]{2,1,0:T(2,128)(2,1)} reshape(bf16[16,2,40960]{2,1,0:T(2,128)(2,1)S(1)} %all_to_all.15) | data formatting | bytes 5242880
  258.4 2.9 copy.116
  261.7 8.4 %multiply_reduce_fusion.1 = (f32[]{:T(128)}, f32[320,1280]{1,0:T(8,128)}) fusion(bf16[4096,320]{0,1:T(8,128)(2,1)S(1)} %bitcast.268, bf16[1,4096,1280]{2,1,0:T(8,128)(2,1)} %all-gather.7.cloned.1.call-done), kind=kOutput, calls=%fused_computation.72 | convolution fusion | flops 3356262400 | bytes 14745604 | tf_op jit(solution)/shard_map/eti,etd->eid/dot_general | solution.py:148
  270.1 25.2 %psum.7 = f32[1]{0:T(128)} all-reduce(f32[1]{0:T(128)} %bitcast.56), channel_id=1, replica_groups=mesh['dp'=16,'ctx'=16] {'ctx'}, use_global_device_ids=true, to_apply=%region_11.12 | all-reduce | flops 1 | bytes 8 | tf_op jit(solution)/shard_map/psum | solution.py:155
  299.6 2.8 mul.259
  302.4 5.9 copy.100
  308.3 9.2 %fusion.74 = (bf16[1,256,5120]{2,1,0:T(8,128)(2,1)S(1)}, bf16[1,256,5120]{2,1,0:T(8,128)(2,1)}) fusion(f32[1,256,5120]{2,1,0:T(8,128)} %copy.100, bf16[1,256,5120]{2,1,0:T(8,128)(2,1)} %param.17, f32[1,256,5120]{2,1,0:T(8,128)} %get-tuple-element.597, f32[256]{0:T(256)S(1)} %get-tuple-element.601, f32[256,5120]{1,0:T(8,128)} %get-tuple-element.602, ...), kind=kLoop, calls=%fused_computation.91 | loop fusion | flops 17039360 | bytes 23595008 | tf_op jit(solution)/shard_map/mul | solution.py:86
  317.5 2.6 copy.101
  320.1 4.1 fusion.69
  324.4 19.7 %all-gather = f32[16,80,1]{1,2,0:T(1,128)S(1)} all-gather(f32[1,80,1]{1,2,0:T(1,128)S(1)} %exp.74), channel_id=2, replica_groups=mesh['dp'=16,'ctx'=16] {'ctx'}, dimensions={0}, use_global_device_ids=true | all-gather | bytes 5440 | tf_op jit(solution)/shard_map/all_gather | solution.py:14
  344.1 4.4 copy.104
  348.5 18.3 %reduce-scatter.4.cloned.1.call-done = f32[80,320]{1,0:T(8,128)} async-done(((f32[1280,320]{1,0:T(8,128)}), f32[80,320]{1,0:T(8,128)}) %reduce-scatter.4.cloned.1.call-update) | async-done | bytes 102416
  368.6 247.3 %all-gather.9.cloned.1.call-done = f32[1280,64,128]{2,1,0:T(8,128)} async-done(((f32[80,64,128]{2,1,0:T(8,128)}), f32[1280,64,128]{2,1,0:T(8,128)}) %all-gather.9.cloned.1.call-update) | async-done | bytes 41943056 | tf_op jit(solution)/shard_map/all_gather | solution.py:14
  615.9 38.5 %while.49 = (s32[]{:T(128)}, f32[1,80,64,128]{3,2,1,0:T(8,128)S(1)}, s32[]{:T(128)}, f32[16,1,80]{2,1,0:T(1,128)S(1)}, f32[16,1,80,64,128]{4,3,2,1,0:T(8,128)}, ...) while((s32[]{:T(128)}, f32[1,80,64,128]{3,2,1,0:T(8,128)S(1)}, s32[]{:T(128)}, ...), condition=%wide.region_7.8_spmd.clone, body=%wide.region_6.7_spmd.clone.sunk | while | flops 2621448 | bytes 7865447 | solution.py:27
  655.7 3.0 broadcast.143
  658.7 35.6 %while.47 = (s32[]{:T(128)}, f32[10,1,256,8,64]{2,4,3,1,0:T(8,128)}, bf16[10,1,8,64,128]{4,3,2,1,0:T(8,128)(2,1)}, bf16[1,256,128]{2,1,0:T(8,128)(2,1)S(1)}, f32...) while((s32[]{:T(128)}, ...), condition=%wide.region_9.10_spmd, body=%wide.region_8.9_spmd.sunk | while | flops 100925440 | bytes 3106417 | solution.py:69
  659.8 2.4 fusion.98
  694.3 2.9 fusion.65
  697.3 2.8 copy.110
  (189 shorter events, 136.0 us)
Async XLA Ops:
  7.2 9.3 %copy-start.3 = (f32[1,80,256]{2,1,0:T(8,128)S(1)}, f32[1,80,256]{2,1,0:T(8,128)}, u32[]{:S(2)}) copy-start(f32[1,80,256]{2,1,0:T(8,128)} %param.20) | copy-start | bytes 245764
  7.2 132.1 %all-gather.11.cloned.1.call-start = ((), (), s32[]{:S(2)}) async-start(), calls=%async_computation.4 | async-start | bytes 15790080 | tf_op jit(solution)/shard_map/all_gather | solution.py:119
  7.9 253.8 %all-gather.7.cloned.1.call-start = ((), (), s32[]{:S(2)}) async-start(), calls=%async_computation.2 | async-start | bytes 11141120 | tf_op jit(solution)/shard_map/all_gather | solution.py:151
  8.7 358.2 %reduce-scatter.4.cloned.1.call-start = ((), (), s32[]{:S(2)}) async-start(), calls=%async_computation.5 | async-start | bytes 2088960
  16.2 5.1 copy-start
  16.3 5.1 copy-start.2
  83.4 75.7 %copy-start.1 = (bf16[1,256,5120]{2,1,0:T(8,128)(2,1)S(1)}, bf16[1,256,5120]{2,1,0:T(8,128)(2,1)}, u32[]{:S(2)}) copy-start(bf16[1,256,5120]{2,1,0:T(8,128)(2,1)} %param.17) | copy-start | bytes 7864324
  83.4 75.7 %copy-start.4 = (f32[5120]{0:T(1024)S(1)}, f32[5120]{0:T(1024)}, u32[]{:S(2)}) copy-start(f32[5120]{0:T(1024)} %param.23) | copy-start | bytes 61444
  299.4 316.5 %all-gather.9.cloned.1.call-start = ((), (), s32[]{:S(2)}) async-start(), calls=%async_computation.3 | async-start | bytes 44564480 | tf_op jit(solution)/shard_map/all_gather | solution.py:14
Sparse Core Ops, SparseCore 0:
  11.9 127.3 all-gather.10
  141.8 81.8 all-gather.6
  299.5 67.2 reduce-scatter.3
  369.4 246.3 all-gather.8
where the time goes:
time: 710 us; the launch traced here: 707 us
  waiting for transfers between devices  323 us (45%)
  other arithmetic  105 us (15%)
  matrix products  98.3 us (14%)
  local copies, waits for them, and re-layouts  83.5 us (12%)
  blocking collectives  81.6 us (11%)
  between operations  14.6 us (2%)
    all_gather x1, waiting for transfers between devices, carried_in(): everything = jax.tree.map(lambda part: lax.all_gather(part, axis), value)  247 us
    all_gather x1, waiting for transfers between devices, per_device(): lax.all_gather(out_weight, ('dp', 'ctx'), axis=0, tiled=True)  55.9 us
    dot_general x20, matrix products, head_block(): inside = jnp.einsum('egtu,eugp->etgp', mixing, scaled)  48.5 us
    unnamed x21, local copies, waits for them, and re-layouts  39.4 us
    select_n x16, other arithmetic, turn(): return jax.tree.map(lambda a, b: jnp.where(reached, a, b), new, before)  37.7 us
    all_to_all x1, blocking collectives, per_device(): lax.all_to_all(gated, 'ctx', split_axis=2, concat_axis=1, tiled=True)  36.7 us
    unnamed x3, other arithmetic  27.9 us
    psum x1, blocking collectives, per_device(): total_sq = lax.psum(squares, 'ctx')  25.2 us
  transfers between devices with their start and end apart: 4, of which 3 were waited for; matrix products, arithmetic and copies ran while one was open for 27% of the time, Pallas kernels for 0%

commit v1 on v0

v1 whole, which is shorter than its diff:
```python
import functools
import math

import jax
import jax.numpy as jnp
from jax import lax
from jax.experimental import pallas as pl
from jax.experimental.pallas import tpu as pltpu
from jax.sharding import PartitionSpec as P

NORM_EPS = 1e-05
CLIP_EPS = 1e-06
MESH = pl.DeviceIdType.MESH
F32 = jnp.float32
BF16 = jnp.bfloat16
HIGHEST = lax.Precision.HIGHEST

TOK = 256
HALF = 128
STATE = 128
GROUP = 8
LANES = 512
GROUPS = 10
INNER = 5120
MODEL = 1280
CAP = 80.0
SIDE = 4
CTX = 16
OWN = INNER // CTX
WIDE = 384
COLS = MODEL // 16
HALFIN = INNER // 2
VMEM_BYTES = 56 * 1024 * 1024


def params(**extra):
    return pltpu.CompilerParams(vmem_limit_bytes=VMEM_BYTES, **extra)


def dot(a, b):
    return jnp.dot(a, b, preferred_element_type=F32)


def dot_nt(a, b):
    return lax.dot_general(a, b, (((1,), (1,)), ((), ())), preferred_element_type=F32)


def dot_tn(a, b):
    return lax.dot_general(a, b, (((0,), (0,)), ((), ())), preferred_element_type=F32)


def rows_of(shape):
    return lax.broadcasted_iota(jnp.int32, shape, 0)


def lanes_of(shape):
    return lax.broadcasted_iota(jnp.int32, shape, 1)


def decay_rows(step, log_rate, upper):
    drop = -(jnp.exp(log_rate) * step)
    cumulative = jnp.dot(drop, upper, preferred_element_type=F32, precision=HIGHEST)
    return cumulative, cumulative - jnp.log(step)


def upper_ones():
    shape = (TOK, TOK)
    return jnp.where(rows_of(shape) <= lanes_of(shape), 1.0, 0.0).astype(F32)


def pair_cols(columns, pair):
    low = lanes_of((TOK, HALF)) < HALF // 2
    return jnp.where(low, columns[:, 2 * pair : 2 * pair + 1], columns[:, 2 * pair + 1 : 2 * pair + 2])


def silu(gate):
    return gate / (1.0 + jnp.exp(-gate))


def forward_kernel(
    x_ref, z_ref, st_ref, lr_ref, s_ref, b_ref, c_ref, gain_ref, gated_ref, r_ref, mixed, coup, upper, acc
):
    at = pl.program_id(0)

    @pl.when(at == 0)
    def _():
        shape = (TOK, TOK)
        both = dot_nt(c_ref[...], b_ref[...])
        coup[...] = jnp.where(rows_of(shape) >= lanes_of(shape), both, 0.0)
        upper[...] = upper_ones()
        acc[...] = jnp.zeros_like(acc)

    cumulative, shifted = decay_rows(st_ref[...], lr_ref[...], upper[...])
    columns = cumulative.T
    low = lanes_of((TOK, HALF)) < HALF // 2
    for pair in range(GROUP // 2):
        lanes = slice(pair * HALF, (pair + 1) * HALF)
        x_pair = x_ref[:, lanes]
        zero = jnp.zeros_like(x_pair)
        parts = (jnp.where(low, x_pair, zero), jnp.where(low, zero, x_pair))
        top = bottom = None
        for which in range(2):
            head = 2 * pair + which
            col = columns[:, head : head + 1]
            row = shifted[head : head + 1, :]
            m_top = jnp.exp(jnp.minimum(col[:HALF] - row[:, :HALF], CAP)) * coup[:HALF, :HALF]
            m_bot = jnp.exp(jnp.minimum(col[HALF:] - row, CAP)) * coup[HALF:, :]
            t = dot(m_top.astype(BF16), parts[which][:HALF])
            b = dot(m_bot.astype(BF16), parts[which])
            top = t if top is None else top + t
            bottom = b if bottom is None else bottom + b
        inside = jnp.concatenate([top, bottom], axis=0)
        carried = dot_nt(c_ref[...], s_ref[lanes, :])
        y = inside + carried * jnp.exp(pair_cols(columns, pair))
        mix = y * silu(z_ref[:, lanes].astype(F32))
        mixed[at, :, lanes] = mix
        acc[...] += mix * mix

    @pl.when(at == GROUPS - 1)
    def _():
        mean = jnp.sum(acc[...], axis=1, keepdims=True) * (1.0 / INNER)
        r = lax.rsqrt(mean + NORM_EPS)
        r_ref[...] = jnp.broadcast_to(r, r_ref.shape)
        for g in range(GROUPS):
            lanes = slice(g * LANES, (g + 1) * LANES)
            gated_ref[:, lanes] = (mixed[g] * r * gain_ref[:, lanes]).astype(BF16)


def forward(x, z, step, log_rate, state, b, c, gain):
    block = lambda i: (0, i)
    whole = lambda i: (0, 0)
    return pl.pallas_call(
        forward_kernel,
        grid=(GROUPS,),
        out_shape=(jax.ShapeDtypeStruct((TOK, INNER), BF16), jax.ShapeDtypeStruct((TOK, HALF), F32)),
        in_specs=[
            pl.BlockSpec((TOK, LANES), block),
            pl.BlockSpec((TOK, LANES), block),
            pl.BlockSpec((GROUP, TOK), lambda i: (i, 0)),
            pl.BlockSpec((GROUP, 1), lambda i: (i, 0)),
            pl.BlockSpec((LANES, STATE), lambda i: (i, 0)),
            pl.BlockSpec((TOK, STATE), whole),
            pl.BlockSpec((TOK, STATE), whole),
            pl.BlockSpec((1, INNER), whole),
        ],
        out_specs=(pl.BlockSpec((TOK, INNER), whole), pl.BlockSpec((TOK, HALF), whole)),
        scratch_shapes=[
            pltpu.VMEM((GROUPS, TOK, LANES), F32),
            pltpu.VMEM((TOK, TOK), F32),
            pltpu.VMEM((TOK, TOK), F32),
            pltpu.VMEM((TOK, HALF), F32),
        ],
        compiler_params=params(),
        cost_estimate=pl.CostEstimate(flops=3 * 10**9, bytes_accessed=10 * 10**6, transcendentals=10**7),
        name="scan_forward",
    )(x, z, step, log_rate, state, b, c, gain)


def norm_kernel(
    og_ref, w_ref, gated_ref, z_ref, r_ref, gain_ref, st_ref, lr_ref, c_ref, yg_ref, push_ref, gg, acc, upper, ct
):
    phase, at = pl.program_id(0), pl.program_id(1)

    @pl.when(jnp.logical_and(phase == 0, at == 0))
    def _():
        acc[...] = jnp.zeros_like(acc)
        upper[...] = upper_ones()
        ct[...] = c_ref[...].astype(F32).T.astype(BF16)

    @pl.when(phase == 0)
    def _():
        value = dot_nt(og_ref[...], w_ref[...])
        gg[at] = value
        product = value * gated_ref[...].astype(F32)
        total = acc[...]
        for i in range(LANES // HALF):
            total += product[:, i * HALF : (i + 1) * HALF]
        acc[...] = total

    @pl.when(phase == 1)
    def _():
        @pl.when(at == 0)
        def _():
            mean = jnp.sum(acc[...], axis=1, keepdims=True) * (1.0 / INNER)
            acc[...] = jnp.broadcast_to(mean, acc.shape)

        cumulative, _ = decay_rows(st_ref[...], lr_ref[...], upper[...])
        columns = cumulative.T
        for pair in range(GROUP // 2):
            lanes = slice(pair * HALF, (pair + 1) * HALF)
            gain = gain_ref[:, lanes]
            inner = gain * gg[at, :, lanes] - gated_ref[:, lanes].astype(F32) * (1.0 / gain) * acc[...]
            yg = silu(z_ref[:, lanes].astype(F32)) * r_ref[...] * inner
            yg_ref[:, lanes] = yg.astype(BF16)
            weighted = (yg * jnp.exp(pair_cols(columns, pair))).astype(BF16)
            push_ref[:, lanes] = dot(ct[...], weighted).astype(BF16)


def norm_backward(og, w, gated, z, r, gain, step, log_rate, c):
    whole = lambda p, i: (0, 0)
    lane = lambda p, i: (0, i)
    late = lambda p, i: (0, i * p)
    late_rows = lambda p, i: (i * p, 0)
    return pl.pallas_call(
        norm_kernel,
        grid=(2, GROUPS),
        out_shape=(jax.ShapeDtypeStruct((TOK, INNER), BF16), jax.ShapeDtypeStruct((STATE, INNER), BF16)),
        in_specs=[
            pl.BlockSpec((TOK, MODEL), whole),
            pl.BlockSpec((LANES, MODEL), lambda p, i: (jnp.where(p == 0, i, GROUPS - 1), 0)),
            pl.BlockSpec((TOK, LANES), lane),
            pl.BlockSpec((TOK, LANES), late),
            pl.BlockSpec((TOK, HALF), whole),
            pl.BlockSpec((1, LANES), late),
            pl.BlockSpec((GROUP, TOK), late_rows),
            pl.BlockSpec((GROUP, 1), late_rows),
            pl.BlockSpec((TOK, STATE), whole),
        ],
        out_specs=(pl.BlockSpec((TOK, LANES), late), pl.BlockSpec((STATE, LANES), late)),
        scratch_shapes=[
            pltpu.VMEM((GROUPS, TOK, LANES), F32),
            pltpu.VMEM((TOK, HALF), F32),
            pltpu.VMEM((TOK, TOK), F32),
            pltpu.VMEM((STATE, TOK), BF16),
        ],
        compiler_params=params(),
        cost_estimate=pl.CostEstimate(flops=4 * 10**9, bytes_accessed=25 * 10**6, transcendentals=3 * 10**6),
        name="norm_backward",
    )(og, w, gated, z, r, gain, step, log_rate, c)


def backward_kernel(yg_ref, sg_ref, st_ref, lr_ref, b_ref, c_ref, out_ref, coup, upper):
    at = pl.program_id(0)

    @pl.when(at == 0)
    def _():
        shape = (TOK, TOK)
        both = dot_nt(b_ref[...], c_ref[...])
        coup[...] = jnp.where(rows_of(shape) <= lanes_of(shape), both, 0.0)
        upper[...] = upper_ones()

    cumulative, shifted = decay_rows(st_ref[...], lr_ref[...], upper[...])
    columns = shifted.T
    last = (cumulative[:, TOK - 1 :] - shifted).T
    low = lanes_of((TOK, HALF)) < HALF // 2
    for pair in range(GROUP // 2):
        lanes = slice(pair * HALF, (pair + 1) * HALF)
        yg = yg_ref[:, lanes]
        zero = jnp.zeros_like(yg)
        parts = (jnp.where(low, yg, zero), jnp.where(low, zero, yg))
        top = bottom = None
        for which in range(2):
            head = 2 * pair + which
            col = columns[:, head : head + 1]
            row = cumulative[head : head + 1, :]
            m_top = jnp.exp(jnp.minimum(row - col[:HALF], CAP)) * coup[:HALF, :]
            m_bot = jnp.exp(jnp.minimum(row[:, HALF:] - col[HALF:], CAP)) * coup[HALF:, HALF:]
            t = dot(m_top.astype(BF16), parts[which])
            b = dot(m_bot.astype(BF16), parts[which][HALF:])
            top = t if top is None else top + t
            bottom = b if bottom is None else bottom + b
        inside = jnp.concatenate([top, bottom], axis=0)
        ended = dot(b_ref[...], sg_ref[:, lanes])
        out_ref[:, lanes] = (inside + ended * jnp.exp(pair_cols(last, pair))).astype(BF16)


def scan_backward(yg, sg, step, log_rate, b, c):
    block = lambda i: (0, i)
    whole = lambda i: (0, 0)
    return pl.pallas_call(
        backward_kernel,
        grid=(GROUPS,),
        out_shape=jax.ShapeDtypeStruct((TOK, INNER), BF16),
        in_specs=[
            pl.BlockSpec((TOK, LANES), block),
            pl.BlockSpec((STATE, LANES), block),
            pl.BlockSpec((GROUP, TOK), lambda i: (i, 0)),
            pl.BlockSpec((GROUP, 1), lambda i: (i, 0)),
            pl.BlockSpec((TOK, STATE), whole),
            pl.BlockSpec((TOK, STATE), whole),
        ],
        out_specs=pl.BlockSpec((TOK, LANES), block),
        scratch_shapes=[pltpu.VMEM((TOK, TOK), F32), pltpu.VMEM((TOK, TOK), F32)],
        compiler_params=params(),
        cost_estimate=pl.CostEstimate(flops=3 * 10**9, bytes_accessed=8 * 10**6, transcendentals=10**7),
        name="scan_backward",
    )(yg, sg, step, log_rate, b, c)


def weight_kernel(*refs):
    gs, os, out_ref = refs[:SIDE], refs[SIDE : 2 * SIDE], refs[2 * SIDE]
    for chunk in range(SIDE):
        total = None
        for g, o in zip(gs, os):
            part = dot_tn(g[:, chunk * OWN : (chunk + 1) * OWN], o[...])
            total = part if total is None else total + part
        out_ref[chunk] = total.astype(BF16)


def weight_partials(gs, os):
    return pl.pallas_call(
        weight_kernel,
        out_shape=jax.ShapeDtypeStruct((SIDE, OWN, MODEL), BF16),
        compiler_params=params(),
        cost_estimate=pl.CostEstimate(flops=4 * 10**9, bytes_accessed=9 * 10**6, transcendentals=0),
        name="weight_partials",
    )(*gs, *os)


def exchange_kernel(
    scale,
    push_ref,
    fac_ref,
    t0_ref,
    t1_ref,
    t2_ref,
    t3_ref,
    sg_ref,
    out_ref,
    arrived,
    facs,
    running,
    spread,
    back,
    landed,
    squares,
    square_own,
    turned,
    chunks,
    paired,
    zsend,
    zrecv,
    p_send,
    p_recv,
    f_send,
    f_recv,
    b_send,
    b_recv,
    q_send,
    q_recv,
    pair_send,
    pair_recv,
    z_send,
    z_recv,
):
    dp, me = lax.axis_index("dp"), lax.axis_index("ctx")
    core, z = lax.rem(dp, 2), lax.div(dp, 2)
    partner = dp + 1 - 2 * core

    barrier = pltpu.get_barrier_semaphore()

    def greet(s, carry):
        pl.semaphore_signal(barrier, inc=1, device_id=(dp, lax.rem(me + s, CTX)), device_id_type=MESH)
        return carry

    def greet_z(s, carry):
        other = 2 * lax.rem(z + s, 8) + core
        pl.semaphore_signal(barrier, inc=1, device_id=(other, me), device_id_type=MESH)
        return carry

    lax.fori_loop(1, CTX, greet, 0)
    lax.fori_loop(1, 8, greet_z, 0)
    pl.semaphore_signal(barrier, inc=1, device_id=(partner, me), device_id_type=MESH)
    pl.semaphore_wait(barrier, CTX - 1 + 7 + 1)

    def piece(ref, owner):
        row = pl.multiple_of(lax.div(owner, 2) * 16, 16)
        lane = pl.multiple_of(lax.rem(owner, 2) * HALFIN, HALFIN)
        return ref.at[pl.ds(row, 16), pl.ds(lane, HALFIN)]

    def push_copy(src, to, slot):
        return pltpu.make_async_remote_copy(
            src_ref=piece(push_ref, src),
            dst_ref=arrived.at[slot],
            send_sem=p_send.at[to],
            recv_sem=p_recv.at[slot],
            device_id=(dp, to),
            device_id_type=MESH,
        )

    def fac_copy(to, slot):
        return pltpu.make_async_remote_copy(
            src_ref=fac_ref,
            dst_ref=facs.at[slot],
            send_sem=f_send.at[to],
            recv_sem=f_recv.at[slot],
            device_id=(dp, to),
            device_id_type=MESH,
        )

    def back_copy(to, owner):
        return pltpu.make_async_remote_copy(
            src_ref=back.at[to],
            dst_ref=piece(landed, owner),
            send_sem=b_send.at[to],
            recv_sem=b_recv.at[owner],
            device_id=(dp, to),
            device_id_type=MESH,
        )

    def square_copy(to, slot):
        return pltpu.make_async_remote_copy(
            src_ref=square_own,
            dst_ref=squares.at[slot],
            send_sem=q_send.at[to],
            recv_sem=q_recv.at[slot],
            device_id=(dp, to),
            device_id_type=MESH,
        )

    pair_copy = pltpu.make_async_remote_copy(
        src_ref=chunks.at[1 - core],
        dst_ref=paired,
        send_sem=pair_send,
        recv_sem=pair_recv,
        device_id=(partner, me),
        device_id_type=MESH,
    )

    def z_copy(to, slot):
        return pltpu.make_async_remote_copy(
            src_ref=zsend.at[to],
            dst_ref=zrecv.at[slot],
            send_sem=z_send.at[to],
            recv_sem=z_recv.at[slot],
            device_id=(2 * to + core, me),
            device_id_type=MESH,
        )

    def others(body):
        def turn(s, carry):
            body(lax.rem(me + s, CTX))
            return carry

        lax.fori_loop(1, CTX, turn, 0)

    def send_pushed(to):
        fac_copy(to, me).start()
        push_copy(to, to, me).start()

    others(send_pushed)

    total = t0_ref[...].astype(F32) + t1_ref[...].astype(F32) + t2_ref[...].astype(F32) + t3_ref[...].astype(F32)
    turned[...] = jnp.zeros_like(turned)
    turned[:OWN, :] = total
    square_own[...] = jnp.sum(jnp.sum((total * total).reshape(OWN // 8, 8, MODEL), axis=0).reshape(8, 10, 128), axis=1)
    others(lambda to: square_copy(to, me).start())

    arrived[me] = piece(push_ref, me)[...]
    facs[me] = fac_ref[...]
    others(lambda k: fac_copy(k, k).wait_recv())
    shape = (HALF, HALFIN)
    head = lax.shift_right_logical(lanes_of(shape) + lax.rem(me, 2) * HALFIN, 6)
    hot = jnp.where(rows_of(shape) == head, 1.0, 0.0).astype(F32)
    listed = jnp.concatenate([facs[k][:1, :] for k in range(CTX)], axis=0)
    wide = jnp.dot(listed, hot, preferred_element_type=F32, precision=HIGHEST)
    for k in range(CTX):
        spread[k] = jnp.broadcast_to(wide[k : k + 1], (8, HALFIN))
    running[...] = jnp.zeros_like(running)

    def chain(turn, carry):
        k = CTX - 1 - turn

        @pl.when(k != me)
        def _():
            push_copy(k, k, k).wait_recv()

        now = running[...]
        back[k] = now.astype(BF16)

        @pl.when(k != me)
        def _():
            back_copy(k, me).start()

        factor = spread[k]
        running[...] = jnp.concatenate([factor, factor], axis=0) * now + arrived[k].astype(F32)
        return carry

    lax.fori_loop(0, CTX, chain, 0)
    piece(landed, me)[...] = back[me]

    others(lambda k: square_copy(k, k).wait_recv())
    squares[me] = square_own[...]
    all_squares = squares[0]
    for k in range(1, CTX):
        all_squares += squares[k]
    whole = jnp.sum(jnp.sum(all_squares, axis=1, keepdims=True), axis=0, keepdims=True)
    clip = jnp.minimum(1.0, lax.rsqrt(whole + CLIP_EPS)) * scale
    for i in range(MODEL // HALF):
        block = (turned[:, i * HALF : (i + 1) * HALF] * clip).T
        lo = i * HALF
        while lo < (i + 1) * HALF:
            owner = lo // COLS
            hi = min((i + 1) * HALF, (owner + 1) * COLS)
            at = slice(lo - owner * COLS, hi - owner * COLS)
            chunks[owner % 2, owner // 2, at] = block[lo - i * HALF : hi - i * HALF].astype(BF16)
            lo = hi
    pair_copy.start()
    pair_copy.wait_recv()

    def add_pair(i, carry):
        zsend[i] = (chunks[core, i].astype(F32) + paired[i].astype(F32)).astype(BF16)
        return carry

    lax.fori_loop(0, 8, add_pair, 0)

    def z_others(body):
        def turn(s, carry):
            body(lax.rem(z + s, 8))
            return carry

        lax.fori_loop(1, 8, turn, 0)

    z_others(lambda to: z_copy(to, z).start())
    others(lambda k: back_copy(me, k).wait_recv())
    sg_ref[...] = landed[...]
    z_others(lambda k: z_copy(k, k).wait_recv())
    zrecv[z] = zsend[z]
    summed = zrecv[0].astype(F32)
    for k in range(1, 8):
        summed += zrecv[k].astype(F32)
    padded = jnp.concatenate([summed, jnp.zeros((HALF - COLS, WIDE), F32)], axis=0).T
    out_ref[...] = padded[:OWN, :COLS]

    def finish(to):
        fac_copy(to, me).wait_send()
        push_copy(to, to, me).wait_send()
        square_copy(to, me).wait_send()
        back_copy(to, me).wait_send()

    others(finish)
    pair_copy.wait_send()
    z_others(lambda to: z_copy(to, z).wait_send())


def exchange(pushed, factors, terms, scale):
    vmem = pl.BlockSpec(memory_space=pltpu.VMEM)
    return pl.pallas_call(
        functools.partial(exchange_kernel, scale),
        out_shape=(jax.ShapeDtypeStruct((STATE, INNER), BF16), jax.ShapeDtypeStruct((OWN, COLS), F32)),
        in_specs=[vmem] * 6,
        out_specs=(vmem, vmem),
        scratch_shapes=[
            pltpu.VMEM((CTX, 16, HALFIN), BF16),
            pltpu.VMEM((CTX, 8, HALF), F32),
            pltpu.VMEM((16, HALFIN), F32),
            pltpu.VMEM((CTX, 8, HALFIN), F32),
            pltpu.VMEM((CTX, 16, HALFIN), BF16),
            pltpu.VMEM((STATE, INNER), BF16),
            pltpu.VMEM((CTX, 8, HALF), F32),
            pltpu.VMEM((8, HALF), F32),
            pltpu.VMEM((WIDE, MODEL), F32),
            pltpu.VMEM((2, 8, COLS, WIDE), BF16),
            pltpu.VMEM((8, COLS, WIDE), BF16),
            pltpu.VMEM((8, COLS, WIDE), BF16),
            pltpu.VMEM((8, COLS, WIDE), BF16),
        ]
        + [pltpu.SemaphoreType.DMA((CTX,))] * 8
        + [pltpu.SemaphoreType.DMA, pltpu.SemaphoreType.DMA]
        + [pltpu.SemaphoreType.DMA((8,))] * 2,
        compiler_params=params(collective_id=0, has_side_effects=True),
        cost_estimate=pl.CostEstimate(flops=10**8, bytes_accessed=50 * 10**6, transcendentals=0),
        name="exchange",
    )(pushed, factors, *terms)


def move(value, axis, step):
    def source(i):
        return (i // SIDE, i % SIDE)

    pairs = []
    for i in range(CTX):
        x, y = source(i)
        to = ((x + step) % SIDE) * SIDE + y if axis == 0 else x * SIDE + (y + step) % SIDE
        pairs.append((i, to))
    return lax.ppermute(value, "ctx", pairs)


def per_device(
    ssm_input,
    gate_input,
    input_map,
    output_map,
    step_size,
    log_rate,
    entry_state,
    norm_gain,
    out_weight,
    out_grad,
):
    examples = lax.axis_size("dp")
    me = lax.axis_index("ctx")
    x, y = me // SIDE, me % SIDE
    ssm, gate, og = ssm_input[0], gate_input[0], out_grad[0]
    b, c, step = input_map[0], output_map[0], step_size[0]
    rates = log_rate.reshape(-1, 1)
    state = entry_state.reshape(INNER, STATE)
    gain = norm_gain.reshape(1, INNER)

    weights = lax.all_gather(out_weight, ("dp", "ctx"), axis=0, tiled=True)
    grads = [og] + [move(og, 0, s) for s in range(1, SIDE)]

    gated, r = forward(ssm, gate, step, rates, state, b, c, gain)
    factor = jnp.exp(-jnp.exp(log_rate) * jnp.sum(step, axis=-1))
    factors = jnp.broadcast_to(jnp.pad(factor, (0, HALF - factor.shape[0]))[None], (8, HALF))

    def columns(s):
        return lax.dynamic_slice_in_dim(gated, lax.rem(x + s, SIDE) * MODEL, MODEL, axis=1)

    gates = [columns(0)] + [move(columns(s), 0, s) for s in range(1, SIDE)]
    partial = weight_partials(gates, grads)

    def chunk(s):
        return lax.dynamic_index_in_dim(partial, lax.rem(y + s, SIDE), axis=0, keepdims=False)

    terms = [chunk(0)] + [move(chunk(s), 1, s) for s in range(1, SIDE)]

    y_grad, pushed = norm_backward(og, weights, gated, gate, r, gain, step, rates, c)
    scale = math.sqrt(INNER * MODEL / examples)
    state_grad, summed = exchange(pushed, factors, terms, scale)
    input_grad = scan_backward(y_grad, state_grad, step, rates, b, c)
    return (input_grad[None], summed)


def solution(mesh):
    placed = (
        P("dp", "ctx", None),
        P("dp", "ctx", None),
        P("dp", "ctx", None),
        P("dp", "ctx", None),
        P("dp", None, "ctx"),
        P(),
        P("dp", "ctx", None, None, None),
        P(),
        P(("dp", "ctx"), None),
        P("dp", "ctx", None),
    )
    return jax.shard_map(
        per_device,
        mesh=mesh,
        in_specs=placed,
        out_specs=(P("dp", "ctx", None), P("ctx", "dp")),
        check_vma=False,
    )
```

time: 710 us -> 306 us (0.43)
  waiting for transfers between devices: 323 us -> 133 us
  Pallas kernels: 0 us -> 113 us
  other arithmetic: 105 us -> 0.11 us
  matrix products: 98.3 us -> 0 us
  blocking collectives: 81.6 us -> 0 us
  local copies, waits for them, and re-layouts: 83.5 us -> 29.4 us
  starting transfers between devices: 0.16 us -> 10.8 us
    all_gather x3 -> x1, waiting for transfers between devices: 303 us -> 72.1 us  [per_device(): weights = lax.all_gather(out_weight, ('dp', 'ctx'), axis=0, tiled=True)]
    pallas_call x0 -> x5, Pallas kernels: none -> 113 us  [the longest x1 49 us: exchange(): pl.pallas_call(functools.partial(exchange_kernel, scale), out_shape=(jax....]
    dot_general x44 -> x0, matrix products: 98.3 us -> none  [the longest x20 48.5 us: head_block(): inside = jnp.einsum('egtu,eugp->etgp', mixing, scaled)]
    ppermute x0 -> x9, waiting for transfers between devices: none -> 60.5 us  [move(): return lax.ppermute(value, 'ctx', pairs)]
    select_n x16 -> x0, other arithmetic: 37.7 us -> none  [turn(): return jax.tree.map(lambda a, b: jnp.where(reached, a, b), new, before)]
    all_to_all x1 -> x0, blocking collectives: 36.7 us -> none  [per_device(): lax.all_to_all(gated, 'ctx', split_axis=2, concat_axis=1, tiled=True)]
    unnamed x3 -> x0, other arithmetic: 27.9 us -> none
    psum x1 -> x0, blocking collectives: 25.2 us -> none  [per_device(): total_sq = lax.psum(squares, 'ctx')]
  transfers between devices with their start and end apart: 4 -> 10, of which waited for: 3 -> 5; matrix products, arithmetic and copies ran while one was open for 27% -> 9% of each run, Pallas kernels for 0% -> 16%
where the time goes in v1:
time: 306 us; the launch traced here: 301 us
  waiting for transfers between devices  133 us (43%)
  Pallas kernels  113 us (37%)
  local copies, waits for them, and re-layouts  29.4 us (10%)
  between operations  14.2 us (5%)
  starting transfers between devices  10.8 us (4%)
    all_gather x1, waiting for transfers between devices, per_device(): weights = lax.all_gather(out_weight, ('dp', 'ctx'), axis=0, tiled=True)  72.1 us
    ppermute x9, waiting for transfers between devices, move(): return lax.ppermute(value, 'ctx', pairs)  60.5 us
    pallas_call x1, Pallas kernels, exchange(): pl.pallas_call(functools.partial(exchange_kernel, scale), out_shape=(jax....  49 us
    pallas_call x1, Pallas kernels, norm_backward(): pl.pallas_call(norm_kernel, grid=(2, GROUPS), out_shape=(jax.ShapeDtypeSt...  23.9 us
    unnamed x14, local copies, waits for them, and re-layouts  21.6 us
    pallas_call x1, Pallas kernels, scan_backward(): pl.pallas_call(backward_kernel, grid=(GROUPS,), out_shape=jax.ShapeDtypeS...  16.7 us
    pallas_call x1, Pallas kernels, forward(): pl.pallas_call(forward_kernel, grid=(GROUPS,), out_shape=(jax.ShapeDtypeS...  15.9 us
    ppermute x9, starting transfers between devices, move(): return lax.ppermute(value, 'ctx', pairs)  10.8 us
  transfers between devices with their start and end apart: 10, of which 5 were waited for; matrix products, arithmetic and copies ran while one was open for 9% of the time, Pallas kernels for 16%

profile of v1, /device:TPU:7, one launch (start us, length us, event | category | flops | bytes accessed | tf_op | source)
XLA Modules:
  0.0 301.0 jit_solution(70120443248512573)
XLA Ops:
  7.2 0.0 all-gather.3.cloned.1.call-start
  7.2 0.7 all-gather.3.cloned.1.call-update
  8.0 1.4 copy.20.lr_ref
  9.3 15.9 %scan_forward.1 = (bf16[256,5120]{1,0:T(8,128)(2,1)}, f32[256,128]{1,0:T(8,128)}) custom-call(bf16[256,5120]{1,0:T(8,128)(2,1)} %bitcast.36, bf16[256,5120]{1,0:T(8,128)(2,1)} %bitcast.19, f32[80,256]{1,0:T(8,128)} %bitcast.26, f32[80,1]{1,0:T(8,128)} %copy.20.lr_ref, bf16[5120,128]{1,0:T(8,128)(2,1)} %bitcast.37, bf16[256,128]{1,0:T(8,128)(2,1)} %bitcast.38, ...), custom_call_target="tpu_custom_call" | custom-call | flops 3000000000 | bytes 10000000 | tf_op jit(solution)/shard_map/scan_forward/pallas_call | solution.py:132
  25.2 2.8 constant_dynamic-slice_fusion
  28.0 0.0 collective-permute-start
  28.0 2.3 collective-permute-start.1
  30.3 0.0 collective-permute-start.2
  30.3 2.7 collective-permute-start.3
  33.0 0.0 collective-permute-start.4
  33.0 11.2 %collective-permute-done.refs_1_ = bf16[256,1280]{1,0:T(8,128)(2,1)S(1)} collective-permute-done((bf16[256,1280]{1,0:T(8,128)(2,1)S(1)}, bf16[256,1280]{1,0:T(8,128)(2,1)S(1)}, u32[]{:S(2)}, u32[]{:S(2)}) %collective-permute-start) | collective-permute-done | bytes 655392 | tf_op jit(solution)/shard_map/ppermute | solution.py:576
  44.2 0.5 collective-permute-start.5
  44.7 0.0 collective-permute-done.1.refs_2_
  44.8 19.3 %collective-permute-done.2.refs_3_ = bf16[256,1280]{1,0:T(8,128)(2,1)} collective-permute-done((bf16[256,1280]{1,0:T(8,128)(2,1)S(1)}, bf16[256,1280]{1,0:T(8,128)(2,1)}, u32[]{:S(2)}, u32[]{:S(2)}) %collective-permute-start.2) | collective-permute-done | bytes 655392 | tf_op jit(solution)/shard_map/ppermute | solution.py:576
  64.1 8.3 %collective-permute-done.3.refs_5_ = bf16[256,1280]{1,0:T(8,128)(2,1)} collective-permute-done((bf16[256,1280]{1,0:T(8,128)(2,1)S(1)}, bf16[256,1280]{1,0:T(8,128)(2,1)}, u32[]{:S(2)}, u32[]{:S(2)}) %collective-permute-start.3) | collective-permute-done | bytes 655392 | tf_op jit(solution)/shard_map/ppermute | solution.py:576
  72.4 21.6 %collective-permute-done.5.refs_7_ = bf16[256,1280]{1,0:T(8,128)(2,1)} collective-permute-done((bf16[256,1280]{1,0:T(8,128)(2,1)S(1)}, bf16[256,1280]{1,0:T(8,128)(2,1)}, u32[]{:S(2)}, u32[]{:S(2)}) %collective-permute-start.5) | collective-permute-done | bytes 655392 | tf_op jit(solution)/shard_map/ppermute | solution.py:576
  94.0 7.8 %weight_partials.1 = bf16[4,320,1280]{2,1,0:T(8,128)(2,1)} custom-call(bf16[256,1280]{1,0:T(8,128)(2,1)} %get-tuple-element.27.refs_0_, bf16[256,1280]{1,0:T(8,128)(2,1)} %copy-done.4, bf16[256,1280]{1,0:T(8,128)(2,1)} %copy-done.5, bf16[256,1280]{1,0:T(8,128)(2,1)} %collective-permute-done.2.refs_3_, bf16[256,1280]{1,0:T(8,128)(2,1)} %bitcast.21, ...), custom_call_target="tpu_custom_call" | custom-call | flops 4000000000 | bytes 9000000 | tf_op jit(solution)/shard_map/weight_partials/pallas_call | solution.py:301
  101.8 3.1 %dynamic-slice_bitcast_fusion = (bf16[320,1280]{1,0:T(8,128)(2,1)S(1)}, bf16[320,1280]{1,0:T(8,128)(2,1)S(1)}, bf16[320,1280]{1,0:T(8,128)(2,1)S(1)}, bf16[320,1280]{1,0:T(8,128)(2,1)}) fusion(bf16[4,320,1280]{2,1,0:T(8,128)(2,1)} %weight_partials.1, s32[]{:T(128)S(6)} %select_n.45, s32[]{:T(128)S(6)} %select_n.44, s32[]{:T(128)S(6)} %select_n.43, s32[]{:T(128)S(6)} %select_n.42), kind=kLoop, calls=%fused_computation | loop fusion | bytes 6553616 | tf_op jit(solution)/shard_map/jit(dynamic_index_in_dim)/squeeze | solution.py:614
  104.9 1.6 collective-permute-start.6
  106.5 2.6 collective-permute-start.7
  109.0 1.0 collective-permute-start.8
  110.1 0.1 reduce_sum.9
  110.2 72.1 %all-gather.3.cloned.1.call-done = bf16[256,20,1280]{2,1,0:T(8,128)(2,1)} async-done(((bf16[1,20,1280]{2,1,0:T(8,128)(2,1)}), bf16[256,20,1280]{2,1,0:T(8,128)(2,1)}) %all-gather.3.cloned.1.call-update) | async-done | bytes 13107216 | tf_op jit(solution)/shard_map/all_gather | solution.py:600
  182.3 19.7 %reshape.18.w_ref = bf16[5120,1280]{1,0:T(8,128)(2,1)} reshape(bf16[256,20,1280]{2,1,0:T(8,128)(2,1)} %all-gather.3.cloned.1.call-done) | data formatting | bytes 26214400
  202.0 23.9 %norm_backward.1 = (bf16[256,5120]{1,0:T(8,128)(2,1)}, bf16[128,5120]{1,0:T(8,128)(2,1)}) custom-call(bf16[256,1280]{1,0:T(8,128)(2,1)} %bitcast.22, bf16[5120,1280]{1,0:T(8,128)(2,1)} %reshape.18.w_ref, bf16[256,5120]{1,0:T(8,128)(2,1)} %get-tuple-element.8.gated_ref, bf16[256,5120]{1,0:T(8,128)(2,1)} %bitcast.20, f32[256,128]{1,0:T(8,128)} %get-tuple-element.9.r_ref, ...), custom_call_target="tpu_custom_call" | custom-call | flops 4000000000 | bytes 25000000 | tf_op jit(solution)/shard_map/norm_backward/pallas_call | solution.py:204
  225.9 0.0 copy-start
  225.9 0.0 collective-permute-done.8.t3_ref
  225.9 0.6 broadcast_in_dim.4.fac_ref
  226.6 0.2 copy-done
  226.8 49.0 %exchange.1 = (bf16[128,5120]{1,0:T(8,128)(2,1)}, f32[320,80]{1,0:T(8,128)}) custom-call(bf16[128,5120]{1,0:T(8,128)(2,1)} %get-tuple-element.11.push_ref, f32[8,128]{1,0:T(8,128)} %broadcast_in_dim.4.fac_ref, bf16[320,1280]{1,0:T(8,128)(2,1)} %get-tuple-element.23.t0_ref, bf16[320,1280]{1,0:T(8,128)(2,1)} %copy-done, ...), custom_call_target="tpu_custom_call" | custom-call | flops 100000000 | bytes 50000000 | tf_op jit(solution)/shard_map/exchange/pallas_call | solution.py:538
  275.8 1.7 copy.23
  277.5 16.7 %scan_backward.1 = bf16[256,5120]{1,0:T(8,128)(2,1)} custom-call(bf16[256,5120]{1,0:T(8,128)(2,1)} %get-tuple-element.10.yg_ref, bf16[128,5120]{1,0:T(8,128)(2,1)} %get-tuple-element.12.sg_ref, f32[80,256]{1,0:T(8,128)} %bitcast.28, f32[80,1]{1,0:T(8,128)} %copy.20.lr_ref, bf16[256,128]{1,0:T(8,128)(2,1)} %bitcast.39, bf16[256,128]{1,0:T(8,128)(2,1)} %bitcast.31), custom_call_target="tpu_custom_call" | custom-call | flops 3000000000 | bytes 8000000 | tf_op jit(solution)/shard_map/scan_backward/pallas_call | solution.py:270
  (15 shorter events, 0.0 us)
Async XLA Ops:
  7.2 175.2 %all-gather.3.cloned.1.call-start = ((), (), s32[]{:S(2)}) async-start(), calls=%async_computation | async-start | bytes 15790080 | tf_op jit(solution)/shard_map/all_gather | solution.py:600
  25.2 5.1 %copy-start.1 = (bf16[1,256,1280]{2,1,0:T(8,128)(2,1)S(1)}, bf16[1,256,1280]{2,1,0:T(8,128)(2,1)}, u32[]{:S(2)}) copy-start(bf16[1,256,1280]{2,1,0:T(8,128)(2,1)} %param.19) | copy-start | bytes 1966084
  28.0 16.3 %collective-permute-start = (bf16[256,1280]{1,0:T(8,128)(2,1)S(1)}, bf16[256,1280]{1,0:T(8,128)(2,1)S(1)}, u32[]{:S(2)}, u32[]{:S(2)}) collective-permute-start(bf16[256,1280]{1,0:T(8,128)(2,1)S(1)} %get-tuple-element.26), channel_id=1, source_target_pairs={{0,4},{1,5},{2,6},{3,7},{4,8},{5,9},{6,10},{7,11},{8,12},{9,13},{1... | collective-permute-start | bytes 1966088 | tf_op jit(solution)/shard_map/ppermute | solution.py:576
  28.0 16.8 %collective-permute-start.1 = (bf16[256,1280]{1,0:T(8,128)(2,1)S(1)}, bf16[256,1280]{1,0:T(8,128)(2,1)S(1)}, u32[]{:S(2)}, u32[]{:S(2)}) collective-permute-start(bf16[256,1280]{1,0:T(8,128)(2,1)S(1)} %get-tuple-element.25), channel_id=1, source_target_pairs={{0,8},{1,9},{2,10},{3,11},{4,12},{5,13},{6,14},{7,15},{8,0},{9,1},... | collective-permute-start | bytes 1966088 | tf_op jit(solution)/shard_map/ppermute | solution.py:576
  30.3 33.8 %collective-permute-start.2 = (bf16[256,1280]{1,0:T(8,128)(2,1)S(1)}, bf16[256,1280]{1,0:T(8,128)(2,1)}, u32[]{:S(2)}, u32[]{:S(2)}) collective-permute-start(bf16[256,1280]{1,0:T(8,128)(2,1)S(1)} %get-tuple-element.24), channel_id=1, source_target_pairs={{0,12},{1,13},{2,14},{3,15},{4,0},{5,1},{6,2},{7,3},{8,4},{9,5},{1... | collective-permute-start | bytes 1966088 | tf_op jit(solution)/shard_map/ppermute | solution.py:576
  30.3 42.1 %collective-permute-start.3 = (bf16[256,1280]{1,0:T(8,128)(2,1)S(1)}, bf16[256,1280]{1,0:T(8,128)(2,1)}, u32[]{:S(2)}, u32[]{:S(2)}) collective-permute-start(bf16[256,1280]{1,0:T(8,128)(2,1)S(1)} %bitcast.23), channel_id=1, source_target_pairs={{0,4},{1,5},{2,6},{3,7},{4,8},{5,9},{6,10},{7,11},{8,12},{9,13},{1... | collective-permute-start | bytes 1966088 | tf_op jit(solution)/shard_map/ppermute | solution.py:576
  33.0 39.4 %collective-permute-start.4 = (bf16[256,1280]{1,0:T(8,128)(2,1)S(1)}, bf16[256,1280]{1,0:T(8,128)(2,1)}, u32[]{:S(2)}, u32[]{:S(2)}) collective-permute-start(bf16[256,1280]{1,0:T(8,128)(2,1)S(1)} %bitcast.24), channel_id=1, source_target_pairs={{0,8},{1,9},{2,10},{3,11},{4,12},{5,13},{6,14},{7,15},{8,0},{9,1},... | collective-permute-start | bytes 1966088 | tf_op jit(solution)/shard_map/ppermute | solution.py:576
  44.2 49.8 %copy-start.4 = (bf16[256,1280]{1,0:T(8,128)(2,1)}, bf16[256,1280]{1,0:T(8,128)(2,1)S(1)}, u32[]{:S(2)}) copy-start(bf16[256,1280]{1,0:T(8,128)(2,1)S(1)} %collective-permute-done.refs_1_) | copy-start | bytes 1966084
  44.2 49.8 %collective-permute-start.5 = (bf16[256,1280]{1,0:T(8,128)(2,1)S(1)}, bf16[256,1280]{1,0:T(8,128)(2,1)}, u32[]{:S(2)}, u32[]{:S(2)}) collective-permute-start(bf16[256,1280]{1,0:T(8,128)(2,1)S(1)} %bitcast.25), channel_id=1, source_target_pairs={{0,12},{1,13},{2,14},{3,15},{4,0},{5,1},{6,2},{7,3},{8,4},{9,5},{1... | collective-permute-start | bytes 1966088 | tf_op jit(solution)/shard_map/ppermute | solution.py:576
  44.8 49.3 %copy-start.5 = (bf16[256,1280]{1,0:T(8,128)(2,1)}, bf16[256,1280]{1,0:T(8,128)(2,1)S(1)}, u32[]{:S(2)}) copy-start(bf16[256,1280]{1,0:T(8,128)(2,1)S(1)} %collective-permute-done.1.refs_2_) | copy-start | bytes 1966084
  101.8 8.3 %copy-start.2 = (f32[1,80,256]{2,1,0:T(8,128)S(1)}, f32[1,80,256]{2,1,0:T(8,128)}, u32[]{:S(2)}) copy-start(f32[1,80,256]{2,1,0:T(8,128)} %param.14) | copy-start | bytes 245764
  101.8 8.4 %copy-start.3 = (f32[80]{0:T(128)S(1)}, f32[80]{0:T(128)}, u32[]{:S(2)}) copy-start(f32[80]{0:T(128)} %param.15) | copy-start | bytes 964
  104.9 121.0 %collective-permute-start.6 = (bf16[320,1280]{1,0:T(8,128)(2,1)S(1)}, bf16[320,1280]{1,0:T(8,128)(2,1)S(1)}, u32[]{:S(2)}, u32[]{:S(2)}) collective-permute-start(bf16[320,1280]{1,0:T(8,128)(2,1)S(1)} %get-tuple-element.22), channel_id=1, source_target_pairs={{0,1},{1,2},{2,3},{3,0},{4,5},{5,6},{6,7},{7,4},{8,9},{9,10},{10,1... | collective-permute-start | bytes 2457608 | tf_op jit(solution)/shard_map/ppermute | solution.py:576
  106.5 119.4 %collective-permute-start.7 = (bf16[320,1280]{1,0:T(8,128)(2,1)S(1)}, bf16[320,1280]{1,0:T(8,128)(2,1)}, u32[]{:S(2)}, u32[]{:S(2)}) collective-permute-start(bf16[320,1280]{1,0:T(8,128)(2,1)S(1)} %get-tuple-element.21), channel_id=1, source_target_pairs={{0,2},{1,3},{2,0},{3,1},{4,6},{5,7},{6,4},{7,5},{8,10},{9,11},{10,... | collective-permute-start | bytes 2457608 | tf_op jit(solution)/shard_map/ppermute | solution.py:576
  109.0 116.9 %collective-permute-start.8 = (bf16[320,1280]{1,0:T(8,128)(2,1)S(1)}, bf16[320,1280]{1,0:T(8,128)(2,1)}, u32[]{:S(2)}, u32[]{:S(2)}) collective-permute-start(bf16[320,1280]{1,0:T(8,128)(2,1)S(1)} %get-tuple-element.20), channel_id=1, source_target_pairs={{0,3},{1,0},{2,1},{3,2},{4,7},{5,4},{6,5},{7,6},{8,11},{9,8},{10,9... | collective-permute-start | bytes 2457608 | tf_op jit(solution)/shard_map/ppermute | solution.py:576
  225.9 0.9 copy-start
Sparse Core Ops, SparseCore 0:
  11.8 170.4 all-gather.2

commit v2 on v1

--- a/solution.py
+++ b/solution.py
@@ -18,9 +18,9 @@
 TOK = 256
 HALF = 128
 STATE = 128
-GROUP = 8
-LANES = 512
-GROUPS = 10
+GROUP = 10
+LANES = 640
+GROUPS = 8
 INNER = 5120
 MODEL = 1280
 CAP = 80.0
@@ -77,156 +77,338 @@
     return gate / (1.0 + jnp.exp(-gate))
 
 
-def forward_kernel(
-    x_ref, z_ref, st_ref, lr_ref, s_ref, b_ref, c_ref, gain_ref, gated_ref, r_ref, mixed, coup, upper, acc
+def gather_kernel(
+    x_ref,
+    z_ref,
+    st_ref,
+    lr_ref,
+    s_ref,
+    b_ref,
+    c_ref,
+    gain_ref,
+    w_ref,
+    og_ref,
+    gated_ref,
+    r_ref,
+    gg_ref,
+    mean_ref,
+    gx_ref,
+    ox_ref,
+    mixed,
+    coup,
+    upper,
+    acc,
+    turned,
+    thin,
+    full,
+    w_send,
+    w_recv,
+    ring_send,
+    ring_recv,
+    sib_send,
+    sib_recv,
+    o_send,
+    o_recv,
+    g_send,
+    g_recv,
 ):
-    at = pl.program_id(0)
-
-    @pl.when(at == 0)
-    def _():
-        shape = (TOK, TOK)
-        both = dot_nt(c_ref[...], b_ref[...])
-        coup[...] = jnp.where(rows_of(shape) >= lanes_of(shape), both, 0.0)
-        upper[...] = upper_ones()
-        acc[...] = jnp.zeros_like(acc)
-
-    cumulative, shifted = decay_rows(st_ref[...], lr_ref[...], upper[...])
-    columns = cumulative.T
-    low = lanes_of((TOK, HALF)) < HALF // 2
-    for pair in range(GROUP // 2):
-        lanes = slice(pair * HALF, (pair + 1) * HALF)
-        x_pair = x_ref[:, lanes]
-        zero = jnp.zeros_like(x_pair)
-        parts = (jnp.where(low, x_pair, zero), jnp.where(low, zero, x_pair))
-        top = bottom = None
-        for which in range(2):
-            head = 2 * pair + which
-            col = columns[:, head : head + 1]
-            row = shifted[head : head + 1, :]
-            m_top = jnp.exp(jnp.minimum(col[:HALF] - row[:, :HALF], CAP)) * coup[:HALF, :HALF]
-            m_bot = jnp.exp(jnp.minimum(col[HALF:] - row, CAP)) * coup[HALF:, :]
-            t = dot(m_top.astype(BF16), parts[which][:HALF])
-            b = dot(m_bot.astype(BF16), parts[which])
-            top = t if top is None else top + t
-            bottom = b if bottom is None else bottom + b
-        inside = jnp.concatenate([top, bottom], axis=0)
-        carried = dot_nt(c_ref[...], s_ref[lanes, :])
-        y = inside + carried * jnp.exp(pair_cols(columns, pair))
-        mix = y * silu(z_ref[:, lanes].astype(F32))
-        mixed[at, :, lanes] = mix
-        acc[...] += mix * mix
-
-    @pl.when(at == GROUPS - 1)
-    def _():
-        mean = jnp.sum(acc[...], axis=1, keepdims=True) * (1.0 / INNER)
-        r = lax.rsqrt(mean + NORM_EPS)
-        r_ref[...] = jnp.broadcast_to(r, r_ref.shape)
-        for g in range(GROUPS):
-            lanes = slice(g * LANES, (g + 1) * LANES)
-            gated_ref[:, lanes] = (mixed[g] * r * gain_ref[:, lanes]).astype(BF16)
-
-
-def forward(x, z, step, log_rate, state, b, c, gain):
-    block = lambda i: (0, i)
-    whole = lambda i: (0, 0)
+    dp, me = lax.axis_index("dp"), lax.axis_index("ctx")
+    core, z = lax.rem(dp, 2), lax.div(dp, 2)
+    x, y = lax.div(me, SIDE), lax.rem(me, SIDE)
+    partner = dp + 1 - 2 * core
+
+    barrier = pltpu.get_barrier_semaphore()
+
+    def greet(s, carry):
+        pl.semaphore_signal(barrier, inc=1, device_id=(dp, lax.rem(me + s, CTX)), device_id_type=MESH)
+        return carry
+
+    lax.fori_loop(1, CTX, greet, 0)
+    for other in (2 * lax.rem(z + 1, 8) + core, 2 * lax.rem(z + 7, 8) + core, partner):
+        pl.semaphore_signal(barrier, inc=1, device_id=(other, me), device_id_type=MESH)
+    pl.semaphore_wait(barrier, CTX - 1 + 3)
+
+    def thin_copy(to, slot):
+        return pltpu.make_async_remote_copy(
+            src_ref=w_ref,
+            dst_ref=thin.at[slot],
+            send_sem=w_send.at[to],
+            recv_sem=w_recv.at[slot],
+            device_id=(dp, to),
+            device_id_type=MESH,
+        )
+
+    def half_block(at, which, half):
+        row = pl.multiple_of(which * OWN + half * (OWN // 2), 16)
+        return full.at[at, pl.ds(row, OWN // 2)]
+
+    def ring_copy(way, turn, half, at):
+        slot = (way * 4 + turn) * 2 + half
+        step = 1 if way == 0 else 7
+        return pltpu.make_async_remote_copy(
+            src_ref=half_block(at, core, half),
+            dst_ref=half_block(at, core, half),
+            send_sem=ring_send.at[slot],
+            recv_sem=ring_recv.at[slot],
+            device_id=(2 * lax.rem(z + step, 8) + core, me),
+            device_id_type=MESH,
+        )
+
+    def sib_copy(at, which, half):
+        return pltpu.make_async_remote_copy(
+            src_ref=half_block(at, which, half),
+            dst_ref=half_block(at, which, half),
+            send_sem=sib_send.at[at, half],
+            recv_sem=sib_recv.at[at, half],
+            device_id=(partner, me),
+            device_id_type=MESH,
+        )
+
+    def o_copy(s, slot):
+        return pltpu.make_async_remote_copy(
+            src_ref=og_ref,
+            dst_ref=ox_ref.at[slot],
+            send_sem=o_send.at[s],
+            recv_sem=o_recv.at[s],
+            device_id=(dp, lax.rem(x + s, SIDE) * SIDE + y),
+            device_id_type=MESH,
+        )
+
+    def g_copy(s, slot):
+        to = lax.rem(x + s, SIDE)
+        return pltpu.make_async_remote_copy(
+            src_ref=turned.at[pl.ds(pl.multiple_of(to * MODEL, MODEL), MODEL)],
+            dst_ref=gx_ref.at[slot],
+            send_sem=g_send.at[s],
+            recv_sem=g_recv.at[s],
+            device_id=(dp, to * SIDE + y),
+            device_id_type=MESH,
+        )
+
+    def others(body):
+        def turn(s, carry):
+            body(lax.rem(me + s, CTX))
+            return carry
+
+        lax.fori_loop(1, CTX, turn, 0)
+
+    others(lambda to: thin_copy(to, me).start())
+    for s in range(1, SIDE):
+        o_copy(s, x).start()
+
+    shape = (TOK, TOK)
+    coup[...] = jnp.where(rows_of(shape) >= lanes_of(shape), dot_nt(c_ref[...], b_ref[...]), 0.0)
+    upper[...] = upper_ones()
+    acc[...] = jnp.zeros_like(acc)
+
+    def group(at, carry):
+        cumulative, shifted = decay_rows(st_ref[at], lr_ref[at], upper[...])
+        columns = cumulative.T
+        low = lanes_of((TOK, HALF)) < HALF // 2
+        for pair in range(GROUP // 2):
+            lanes = pl.ds(pl.multiple_of(at * LANES + pair * HALF, HALF), HALF)
+            x_pair = x_ref[:, lanes]
+            zero = jnp.zeros_like(x_pair)
+            parts = (jnp.where(low, x_pair, zero), jnp.where(low, zero, x_pair))
+            top = bottom = None
+            for which in range(2):
+                head = 2 * pair + which
+                col = columns[:, head : head + 1]
+                row = shifted[head : head + 1, :]
+                m_top = jnp.exp(jnp.minimum(col[:HALF] - row[:, :HALF], CAP)) * coup[:HALF, :HALF]
+                m_bot = jnp.exp(jnp.minimum(col[HALF:] - row, CAP)) * coup[HALF:, :]
+                t = dot(m_top.astype(BF16), parts[which][:HALF])
+                b = dot(m_bot.astype(BF16), parts[which])
+                top = t if top is None else top + t
+                bottom = b if bottom is None else bottom + b
+            inside = jnp.concatenate([top, bottom], axis=0)
+            carried = dot_nt(c_ref[...], s_ref[lanes, :])
+            value = inside + carried * jnp.exp(pair_cols(columns, pair))
+            mix = value * silu(z_ref[:, lanes].astype(F32))
+            mixed[at, :, pair * HALF : (pair + 1) * HALF] = mix
+            acc[...] += mix * mix
+        return carry
+
+    def arrive(turn, half):
+        for way in (0, 1):
+            if turn == 3 and half != way:
+                continue
+            at = lax.rem(z + (8 - turn - 1 if way == 0 else turn + 1), 8)
+            ring_copy(way, turn, half, at).wait_recv()
+            if turn < 2 or (turn == 2 and half == way):
+                ring_copy(way, turn + 1, half, at).start()
+            sib_copy(at, core, half).start()
+
+    lax.fori_loop(0, 2, group, 0)
+
+    thin[me] = w_ref[...]
+    others(lambda k: thin_copy(k, k).wait_recv())
+    rows = [thin[k][: OWN // CTX].astype(F32) for k in range(CTX)]
+    own = pl.ds(pl.multiple_of(core * OWN, 16), OWN)
+    full[z, own] = jnp.concatenate(rows, axis=0).astype(BF16)
+    for half in range(2):
+        for way in range(2):
+            ring_copy(way, 0, half, z).start()
+    for half in range(2):
+        sib_copy(z, core, half).start()
+
+    lax.fori_loop(2, 6, group, 0)
+    arrive(0, 0)
+    lax.fori_loop(6, GROUPS, group, 0)
+    arrive(0, 1)
+
+    r = lax.rsqrt(jnp.sum(acc[...], axis=1, keepdims=True) * (1.0 / INNER) + NORM_EPS)
+    r_ref[...] = jnp.broadcast_to(r, r_ref.shape)
+
+    def finish_norm(at, carry):
+        lanes = pl.ds(pl.multiple_of(at * LANES, HALF), LANES)
+        normed = mixed[at] * r_ref[:, :1] * gain_ref[:, lanes]
+        gated_ref[:, lanes] = normed.astype(BF16)
+        turned[lanes, :] = normed.T.astype(BF16)
+        return carry
+
+    lax.fori_loop(0, GROUPS, finish_norm, 0)
+    for s in range(1, SIDE):
+        g_copy(s, x).start()
+    gx_ref[x] = turned[pl.ds(pl.multiple_of(x * MODEL, MODEL), MODEL), :]
+    ox_ref[x] = og_ref[...]
+    acc[...] = jnp.zeros_like(acc)
+
+    def product(at):
+        for half in range(2):
+            sib_copy(at, 1 - core, half).wait_recv()
+        value = dot_nt(og_ref[...], full[at])
+        gg_ref[at] = value
+        lanes = pl.ds(pl.multiple_of(at * LANES, HALF), LANES)
+        both = value * gated_ref[:, lanes].astype(F32)
+        total = acc[...]
+        for i in range(LANES // HALF):
+            total += both[:, i * HALF : (i + 1) * HALF]
+        acc[...] = total
+
+    arrive(1, 0)
+    product(z)
+    arrive(1, 1)
+    product(lax.rem(z + 1, 8))
+    arrive(2, 0)
+    product(lax.rem(z + 7, 8))
+    arrive(2, 1)
+    product(lax.rem(z + 2, 8))
+    arrive(3, 0)
+    product(lax.rem(z + 6, 8))
+    arrive(3, 1)
+    product(lax.rem(z + 3, 8))
+    product(lax.rem(z + 5, 8))
+    product(lax.rem(z + 4, 8))
+    mean = jnp.sum(acc[...], axis=1, keepdims=True) * (1.0 / INNER)
+    mean_ref[...] = jnp.broadcast_to(mean, mean_ref.shape)
+
+    for s in range(1, SIDE):
+        source = lax.rem(x + SIDE - s, SIDE)
+        o_copy(s, source).wait_recv()
+        g_copy(s, source).wait_recv()
+        o_copy(s, x).wait_send()
+        g_copy(s, x).wait_send()
+    others(lambda to: thin_copy(to, me).wait_send())
+    for turn in range(4):
+        for half in range(2):
+            for way in range(2):
+                if turn == 3 and half != way:
+                    continue
+                at = lax.rem(z + (8 - turn if way == 0 else turn), 8)
+                ring_copy(way, turn, half, at).wait_send()
+
+    def finish(at, carry):
+        for half in range(2):
+            sib_copy(at, core, half).wait_send()
+        return carry
+
+    lax.fori_loop(0, 8, finish, 0)
+
+
+def gather(x, z, step, log_rate, state, b, c, gain, w, og):
+    vmem = pl.BlockSpec(memory_space=pltpu.VMEM)
+    dma = pltpu.SemaphoreType.DMA
     return pl.pallas_call(
-        forward_kernel,
-        grid=(GROUPS,),
-        out_shape=(jax.ShapeDtypeStruct((TOK, INNER), BF16), jax.ShapeDtypeStruct((TOK, HALF), F32)),
-        in_specs=[
-            pl.BlockSpec((TOK, LANES), block),
-            pl.BlockSpec((TOK, LANES), block),
-            pl.BlockSpec((GROUP, TOK), lambda i: (i, 0)),
-            pl.BlockSpec((GROUP, 1), lambda i: (i, 0)),
-            pl.BlockSpec((LANES, STATE), lambda i: (i, 0)),
-            pl.BlockSpec((TOK, STATE), whole),
-            pl.BlockSpec((TOK, STATE), whole),
-            pl.BlockSpec((1, INNER), whole),
-        ],
-        out_specs=(pl.BlockSpec((TOK, INNER), whole), pl.BlockSpec((TOK, HALF), whole)),
+        gather_kernel,
+        out_shape=(
+            jax.ShapeDtypeStruct((TOK, INNER), BF16),
+            jax.ShapeDtypeStruct((TOK, HALF), F32),
+            jax.ShapeDtypeStruct((GROUPS, TOK, LANES), F32),
+            jax.ShapeDtypeStruct((TOK, HALF), F32),
+            jax.ShapeDtypeStruct((SIDE, MODEL, TOK), BF16),
+            jax.ShapeDtypeStruct((SIDE, TOK, MODEL), BF16),
+        ),
+        in_specs=[vmem] * 10,
+        out_specs=(vmem,) * 6,
         scratch_shapes=[
             pltpu.VMEM((GROUPS, TOK, LANES), F32),
             pltpu.VMEM((TOK, TOK), F32),
             pltpu.VMEM((TOK, TOK), F32),
             pltpu.VMEM((TOK, HALF), F32),
+            pltpu.VMEM((INNER, TOK), BF16),
+            pltpu.VMEM((CTX, 32, MODEL), BF16),
+            pltpu.VMEM((8, 2 * OWN, MODEL), BF16),
+            dma((CTX,)),
+            dma((CTX,)),
+            dma((16,)),
+            dma((16,)),
+            dma((8, 2)),
+            dma((8, 2)),
+            dma((SIDE,)),
+            dma((SIDE,)),
+            dma((SIDE,)),
+            dma((SIDE,)),
         ],
-        compiler_params=params(),
-        cost_estimate=pl.CostEstimate(flops=3 * 10**9, bytes_accessed=10 * 10**6, transcendentals=10**7),
-        name="scan_forward",
-    )(x, z, step, log_rate, state, b, c, gain)
-
-
-def norm_kernel(
-    og_ref, w_ref, gated_ref, z_ref, r_ref, gain_ref, st_ref, lr_ref, c_ref, yg_ref, push_ref, gg, acc, upper, ct
-):
-    phase, at = pl.program_id(0), pl.program_id(1)
-
-    @pl.when(jnp.logical_and(phase == 0, at == 0))
+        compiler_params=params(collective_id=1, has_side_effects=True),
+        cost_estimate=pl.CostEstimate(flops=7 * 10**9, bytes_accessed=60 * 10**6, transcendentals=10**7),
+        name="gather",
+    )(x, z, step, log_rate, state, b, c, gain, w, og)
+
+
+def norm_kernel(gg_ref, gated_ref, z_ref, r_ref, mean_ref, gain_ref, st_ref, lr_ref, c_ref, yg_ref, push_ref, upper, ct):
+    @pl.when(pl.program_id(0) == 0)
     def _():
-        acc[...] = jnp.zeros_like(acc)
         upper[...] = upper_ones()
         ct[...] = c_ref[...].astype(F32).T.astype(BF16)
 
-    @pl.when(phase == 0)
-    def _():
-        value = dot_nt(og_ref[...], w_ref[...])
-        gg[at] = value
-        product = value * gated_ref[...].astype(F32)
-        total = acc[...]
-        for i in range(LANES // HALF):
-            total += product[:, i * HALF : (i + 1) * HALF]
-        acc[...] = total
-
-    @pl.when(phase == 1)
-    def _():
-        @pl.when(at == 0)
-        def _():
-            mean = jnp.sum(acc[...], axis=1, keepdims=True) * (1.0 / INNER)
-            acc[...] = jnp.broadcast_to(mean, acc.shape)
-
-        cumulative, _ = decay_rows(st_ref[...], lr_ref[...], upper[...])
-        columns = cumulative.T
-        for pair in range(GROUP // 2):
-            lanes = slice(pair * HALF, (pair + 1) * HALF)
-            gain = gain_ref[:, lanes]
-            inner = gain * gg[at, :, lanes] - gated_ref[:, lanes].astype(F32) * (1.0 / gain) * acc[...]
-            yg = silu(z_ref[:, lanes].astype(F32)) * r_ref[...] * inner
-            yg_ref[:, lanes] = yg.astype(BF16)
-            weighted = (yg * jnp.exp(pair_cols(columns, pair))).astype(BF16)
-            push_ref[:, lanes] = dot(ct[...], weighted).astype(BF16)
-
-
-def norm_backward(og, w, gated, z, r, gain, step, log_rate, c):
-    whole = lambda p, i: (0, 0)
-    lane = lambda p, i: (0, i)
-    late = lambda p, i: (0, i * p)
-    late_rows = lambda p, i: (i * p, 0)
+    cumulative, _ = decay_rows(st_ref[0], lr_ref[0], upper[...])
+    columns = cumulative.T
+    for pair in range(GROUP // 2):
+        lanes = slice(pair * HALF, (pair + 1) * HALF)
+        gain = gain_ref[:, lanes]
+        inner = gain * gg_ref[0, :, lanes] - gated_ref[:, lanes].astype(F32) * (1.0 / gain) * mean_ref[...]
+        yg = silu(z_ref[:, lanes].astype(F32)) * r_ref[...] * inner
+        yg_ref[:, lanes] = yg.astype(BF16)
+        weighted = (yg * jnp.exp(pair_cols(columns, pair))).astype(BF16)
+        push_ref[:, lanes] = dot(ct[...], weighted).astype(BF16)
+
+
+def norm_backward(gg, gated, z, r, mean, gain, step, log_rate, c):
+    whole = lambda i: (0, 0)
+    lane = lambda i: (0, i)
+    lead = lambda i: (i, 0, 0)
     return pl.pallas_call(
         norm_kernel,
-        grid=(2, GROUPS),
+        grid=(GROUPS,),
         out_shape=(jax.ShapeDtypeStruct((TOK, INNER), BF16), jax.ShapeDtypeStruct((STATE, INNER), BF16)),
         in_specs=[
-            pl.BlockSpec((TOK, MODEL), whole),
-            pl.BlockSpec((LANES, MODEL), lambda p, i: (jnp.where(p == 0, i, GROUPS - 1), 0)),
+            pl.BlockSpec((1, TOK, LANES), lead),
             pl.BlockSpec((TOK, LANES), lane),
-            pl.BlockSpec((TOK, LANES), late),
+            pl.BlockSpec((TOK, LANES), lane),
             pl.BlockSpec((TOK, HALF), whole),
-            pl.BlockSpec((1, LANES), late),
-            pl.BlockSpec((GROUP, TOK), late_rows),
-            pl.BlockSpec((GROUP, 1), late_rows),
+            pl.BlockSpec((TOK, HALF), whole),
+            pl.BlockSpec((1, LANES), lane),
+            pl.BlockSpec((1, GROUP, TOK), lead),
+            pl.BlockSpec((1, GROUP, 1), lead),
             pl.BlockSpec((TOK, STATE), whole),
         ],
-        out_specs=(pl.BlockSpec((TOK, LANES), late), pl.BlockSpec((STATE, LANES), late)),
-        scratch_shapes=[
-            pltpu.VMEM((GROUPS, TOK, LANES), F32),
-            pltpu.VMEM((TOK, HALF), F32),
-            pltpu.VMEM((TOK, TOK), F32),
-            pltpu.VMEM((STATE, TOK), BF16),
-        ],
+        out_specs=(pl.BlockSpec((TOK, LANES), lane), pl.BlockSpec((STATE, LANES), lane)),
+        scratch_shapes=[pltpu.VMEM((TOK, TOK), F32), pltpu.VMEM((STATE, TOK), BF16)],
         compiler_params=params(),
-        cost_estimate=pl.CostEstimate(flops=4 * 10**9, bytes_accessed=25 * 10**6, transcendentals=3 * 10**6),
+        cost_estimate=pl.CostEstimate(flops=10**9, bytes_accessed=15 * 10**6, transcendentals=3 * 10**6),
         name="norm_backward",
-    )(og, w, gated, z, r, gain, step, log_rate, c)
+    )(gg, gated, z, r, mean, gain, step, log_rate, c)
 
 
 def backward_kernel(yg_ref, sg_ref, st_ref, lr_ref, b_ref, c_ref, out_ref, coup, upper):
@@ -239,7 +421,7 @@
         coup[...] = jnp.where(rows_of(shape) <= lanes_of(shape), both, 0.0)
         upper[...] = upper_ones()
 
-    cumulative, shifted = decay_rows(st_ref[...], lr_ref[...], upper[...])
+    cumulative, shifted = decay_rows(st_ref[0], lr_ref[0], upper[...])
     columns = shifted.T
     last = (cumulative[:, TOK - 1 :] - shifted).T
     low = lanes_of((TOK, HALF)) < HALF // 2
@@ -274,8 +456,8 @@
         in_specs=[
             pl.BlockSpec((TOK, LANES), block),
             pl.BlockSpec((STATE, LANES), block),
-            pl.BlockSpec((GROUP, TOK), lambda i: (i, 0)),
-            pl.BlockSpec((GROUP, 1), lambda i: (i, 0)),
+            pl.BlockSpec((1, GROUP, TOK), lambda i: (i, 0, 0)),
+            pl.BlockSpec((1, GROUP, 1), lambda i: (i, 0, 0)),
             pl.BlockSpec((TOK, STATE), whole),
             pl.BlockSpec((TOK, STATE), whole),
         ],
@@ -287,12 +469,11 @@
     )(yg, sg, step, log_rate, b, c)
 
 
-def weight_kernel(*refs):
-    gs, os, out_ref = refs[:SIDE], refs[SIDE : 2 * SIDE], refs[2 * SIDE]
+def weight_kernel(g_ref, o_ref, out_ref):
     for chunk in range(SIDE):
         total = None
-        for g, o in zip(gs, os):
-            part = dot_tn(g[:, chunk * OWN : (chunk + 1) * OWN], o[...])
+        for source in range(SIDE):
+            part = dot(g_ref[source, chunk * OWN : (chunk + 1) * OWN, :], o_ref[source])
             total = part if total is None else total + part
         out_ref[chunk] = total.astype(BF16)
 
@@ -304,7 +485,7 @@
         compiler_params=params(),
         cost_estimate=pl.CostEstimate(flops=4 * 10**9, bytes_accessed=9 * 10**6, transcendentals=0),
         name="weight_partials",
-    )(*gs, *os)
+    )(gs, os)
 
 
 def exchange_kernel(
@@ -590,32 +771,26 @@
 ):
     examples = lax.axis_size("dp")
     me = lax.axis_index("ctx")
-    x, y = me // SIDE, me % SIDE
+    y = me % SIDE
     ssm, gate, og = ssm_input[0], gate_input[0], out_grad[0]
-    b, c, step = input_map[0], output_map[0], step_size[0]
-    rates = log_rate.reshape(-1, 1)
+    b, c = input_map[0], output_map[0]
+    step = step_size.reshape(GROUPS, GROUP, TOK)
+    rates = log_rate.reshape(GROUPS, GROUP, 1)
     state = entry_state.reshape(INNER, STATE)
     gain = norm_gain.reshape(1, INNER)
-
-    weights = lax.all_gather(out_weight, ("dp", "ctx"), axis=0, tiled=True)
-    grads = [og] + [move(og, 0, s) for s in range(1, SIDE)]
-
-    gated, r = forward(ssm, gate, step, rates, state, b, c, gain)
-    factor = jnp.exp(-jnp.exp(log_rate) * jnp.sum(step, axis=-1))
+    padded = jnp.pad(out_weight, ((0, 32 - out_weight.shape[0]), (0, 0)))
+
+    gated, r, gg, mean, gx, ox = gather(ssm, gate, step, rates, state, b, c, gain, padded, og)
+    factor = jnp.exp(-jnp.exp(log_rate) * jnp.sum(step_size[0], axis=-1))
     factors = jnp.broadcast_to(jnp.pad(factor, (0, HALF - factor.shape[0]))[None], (8, HALF))
-
-    def columns(s):
-        return lax.dynamic_slice_in_dim(gated, lax.rem(x + s, SIDE) * MODEL, MODEL, axis=1)
-
-    gates = [columns(0)] + [move(columns(s), 0, s) for s in range(1, SIDE)]
-    partial = weight_partials(gates, grads)
+    partial = weight_partials(gx, ox)
 
     def chunk(s):
         return lax.dynamic_index_in_dim(partial, lax.rem(y + s, SIDE), axis=0, keepdims=False)
 
     terms = [chunk(0)] + [move(chunk(s), 1, s) for s in range(1, SIDE)]
 
-    y_grad, pushed = norm_backward(og, weights, gated, gate, r, gain, step, rates, c)
+    y_grad, pushed = norm_backward(gg, gated, gate, r, mean, gain, step, rates, c)
     scale = math.sqrt(INNER * MODEL / examples)
     state_grad, summed = exchange(pushed, factors, terms, scale)
     input_grad = scan_backward(y_grad, state_grad, step, rates, b, c)

time: 306 us -> 243 us (0.79); the launches traced: 301 us -> 243 us
  waiting for transfers between devices: 133 us -> 23 us
  Pallas kernels: 113 us -> 191 us
  local copies, waits for them, and re-layouts: 29.4 us -> 9.74 us
  between operations: 14.2 us -> 0.73 us
  starting transfers between devices: 10.8 us -> 18.5 us
    pallas_call x2, Pallas kernels: 39.7 us -> 114 us  [the longest x1 102 us: gather(): pl.pallas_call(gather_kernel, out_shape=(jax.ShapeDtypeStruct((TOK, INNER...]
    all_gather x1 -> x0, waiting for transfers between devices: 72.1 us -> none  [per_device(): weights = lax.all_gather(out_weight, ('dp', 'ctx'), axis=0, tiled=True)]
    ppermute x9 -> x3, waiting for transfers between devices: 60.5 us -> 23 us  [move(): return lax.ppermute(value, 'ctx', pairs)]
    unnamed x14 -> x7, local copies, waits for them, and re-layouts: 21.6 us -> 1.7 us
    ppermute x9 -> x3, starting transfers between devices: 10.8 us -> 18.5 us  [move(): return lax.ppermute(value, 'ctx', pairs)]
    pallas_call x1, Pallas kernels: 49 us -> 53.7 us  [exchange(): pl.pallas_call(functools.partial(exchange_kernel, scale), out_shape=(jax....]
  transfers between devices with their start and end apart: 10 -> 3, of which waited for: 5 -> 2; matrix products, arithmetic and copies ran while one was open for 9% -> 0% of each run, Pallas kernels for 16% -> 5%
where the time goes in v2:
time: 243 us
  Pallas kernels  191 us (79%)
  waiting for transfers between devices  23 us (9%)
  starting transfers between devices  18.5 us (8%)
  local copies, waits for them, and re-layouts  9.74 us (4%)
    pallas_call x1, Pallas kernels, gather(): pl.pallas_call(gather_kernel, out_shape=(jax.ShapeDtypeStruct((TOK, INNER...  102 us
    pallas_call x1, Pallas kernels, exchange(): pl.pallas_call(functools.partial(exchange_kernel, scale), out_shape=(jax....  53.7 us
    ppermute x3, waiting for transfers between devices, move(): return lax.ppermute(value, 'ctx', pairs)  23 us
    ppermute x3, starting transfers between devices, move(): return lax.ppermute(value, 'ctx', pairs)  18.5 us
    pallas_call x1, Pallas kernels, scan_backward(): pl.pallas_call(backward_kernel, grid=(GROUPS,), out_shape=jax.ShapeDtypeS...  15.1 us
    pallas_call x1, Pallas kernels, norm_backward(): pl.pallas_call(norm_kernel, grid=(GROUPS,), out_shape=(jax.ShapeDtypeStru...  12.3 us
    pallas_call x1, Pallas kernels, weight_partials(): pl.pallas_call(weight_kernel, out_shape=jax.ShapeDtypeStruct((SIDE, OWN,...  7.8 us
  transfers between devices with their start and end apart: 3, of which 2 were waited for; matrix products, arithmetic and copies ran while one was open for 0% of the time, Pallas kernels for 5%

profile of v2, /device:TPU:7, one launch (start us, length us, event | category | flops | bytes accessed | tf_op | source)
XLA Modules:
  0.0 242.8 jit_solution(14560109861144784543)
XLA Ops:
  0.7 1.5 reshape.17.st_ref
  2.2 1.4 reshape.21.lr_ref
  3.6 1.5 pad.8.w_ref
  5.1 101.8 %gather.1 = (bf16[256,5120]{1,0:T(8,128)(2,1)}, f32[256,128]{1,0:T(8,128)}, f32[8,256,640]{2,1,0:T(8,128)}, f32[256,128]{1,0:T(8,128)}, bf16[4,1280,256]{2,1,0:T(8,128)(2,1)}, /*index=5*/bf16[4,256,1280]{2,1,0:T(8,128)(2,1)}) custom-call(bf16[256,5120]{1,0:T(8,128)(2,1)} %bitcast.23, bf16[256,5120]{1,0:T(8,128)(2,1)} %bitcast.16, ...), custom_call_target="tpu_custom_call" | custom-call | flops 7000000000 | bytes 60000000 | tf_op jit(solution)/shard_map/gather/pallas_call | solution.py:332
  106.9 7.8 %weight_partials.1 = bf16[4,320,1280]{2,1,0:T(8,128)(2,1)} custom-call(bf16[4,1280,256]{2,1,0:T(8,128)(2,1)} %get-tuple-element.18.g_ref, bf16[4,256,1280]{2,1,0:T(8,128)(2,1)} %get-tuple-element.19.o_ref), custom_call_target="tpu_custom_call" | custom-call | flops 4000000000 | bytes 9000000 | tf_op jit(solution)/shard_map/weight_partials/pallas_call | solution.py:482
  114.8 0.0 copy-start.1
  114.8 0.0 copy-start.2
  114.8 3.0 %dynamic-slice_bitcast_fusion = (bf16[320,1280]{1,0:T(8,128)(2,1)S(1)}, bf16[320,1280]{1,0:T(8,128)(2,1)S(1)}, bf16[320,1280]{1,0:T(8,128)(2,1)S(1)}, bf16[320,1280]{1,0:T(8,128)(2,1)}) fusion(bf16[4,320,1280]{2,1,0:T(8,128)(2,1)} %weight_partials.1, s32[]{:T(128)S(6)} %select_n.24, s32[]{:T(128)S(6)} %select_n.23, s32[]{:T(128)S(6)} %select_n.22, s32[]{:T(128)S(6)} %select_n.21), kind=kLoop, calls=%fused_computation | loop fusion | bytes 6553616 | tf_op jit(solution)/shard_map/jit(dynamic_index_in_dim)/squeeze | solution.py:789
  117.8 0.0 collective-permute-start
  117.8 18.5 %collective-permute-start.1 = (bf16[320,1280]{1,0:T(8,128)(2,1)S(1)}, bf16[320,1280]{1,0:T(8,128)(2,1)}, u32[]{:S(2)}, u32[]{:S(2)}) collective-permute-start(bf16[320,1280]{1,0:T(8,128)(2,1)S(1)} %get-tuple-element.27), channel_id=1, source_target_pairs={{0,2},{1,3},{2,0},{3,1},{4,6},{5,7},{6,4},{7,5},{8,10},{9,11},{10,... | collective-permute-start | bytes 2457608 | tf_op jit(solution)/shard_map/ppermute | solution.py:757
  136.2 0.0 collective-permute-start.2
  136.2 0.0 copy-done.1
  136.2 0.1 reduce_sum.9
  136.3 0.0 copy-done.2
  136.4 12.3 %norm_backward.1 = (bf16[256,5120]{1,0:T(8,128)(2,1)}, bf16[128,5120]{1,0:T(8,128)(2,1)}) custom-call(f32[8,256,640]{2,1,0:T(8,128)} %get-tuple-element.12.gg_ref, bf16[256,5120]{1,0:T(8,128)(2,1)} %get-tuple-element.13.gated_ref, bf16[256,5120]{1,0:T(8,128)(2,1)} %bitcast.17, f32[256,128]{1,0:T(8,128)} %get-tuple-element.14.r_ref, ...), custom_call_target="tpu_custom_call" | custom-call | flops 1000000000 | bytes 15000000 | tf_op jit(solution)/shard_map/norm_backward/pallas_call | solution.py:391
  148.7 4.5 %collective-permute-done.t1_ref = bf16[320,1280]{1,0:T(8,128)(2,1)S(1)} collective-permute-done((bf16[320,1280]{1,0:T(8,128)(2,1)S(1)}, bf16[320,1280]{1,0:T(8,128)(2,1)S(1)}, u32[]{:S(2)}, u32[]{:S(2)}) %collective-permute-start) | collective-permute-done | bytes 819232 | tf_op jit(solution)/shard_map/ppermute | solution.py:757
  153.2 0.0 copy-start
  153.2 18.5 %collective-permute-done.1.t2_ref = bf16[320,1280]{1,0:T(8,128)(2,1)} collective-permute-done((bf16[320,1280]{1,0:T(8,128)(2,1)S(1)}, bf16[320,1280]{1,0:T(8,128)(2,1)}, u32[]{:S(2)}, u32[]{:S(2)}) %collective-permute-start.1) | collective-permute-done | bytes 819232 | tf_op jit(solution)/shard_map/ppermute | solution.py:757
  171.7 0.0 collective-permute-done.2.t3_ref
  171.7 0.6 broadcast_in_dim.4.fac_ref
  172.3 0.0 copy-done
  172.3 53.7 %exchange.1 = (bf16[128,5120]{1,0:T(8,128)(2,1)}, f32[320,80]{1,0:T(8,128)}) custom-call(bf16[128,5120]{1,0:T(8,128)(2,1)} %get-tuple-element.17.push_ref, f32[8,128]{1,0:T(8,128)} %broadcast_in_dim.4.fac_ref, bf16[320,1280]{1,0:T(8,128)(2,1)} %get-tuple-element.29.t0_ref, bf16[320,1280]{1,0:T(8,128)(2,1)} %copy-done, ...), custom_call_target="tpu_custom_call" | custom-call | flops 100000000 | bytes 50000000 | tf_op jit(solution)/shard_map/exchange/pallas_call | solution.py:719
  226.0 1.7 copy.19
  227.7 15.1 %scan_backward.1 = bf16[256,5120]{1,0:T(8,128)(2,1)} custom-call(bf16[256,5120]{1,0:T(8,128)(2,1)} %get-tuple-element.16.yg_ref, bf16[128,5120]{1,0:T(8,128)(2,1)} %get-tuple-element.20.sg_ref, f32[8,10,256]{2,1,0:T(8,128)} %reshape.17.st_ref, f32[8,10,1]{2,1,0:T(8,128)} %reshape.21.lr_ref, bf16[256,128]{1,0:T(8,128)(2,1)} %bitcast.27, bf16[256,128]{1,0:T(8,128)(2,1)} %bitcast.20), custom_call_target="tpu_custom_call" | custom-call | flops 3000000000 | bytes 8000000 | tf_op jit(solution)/shard_map/scan_backward/pallas_call | solution.py:452
  (2 shorter events, 0.0 us)
Async XLA Ops:
  114.8 21.5 %copy-start.1 = (f32[1,80,256]{2,1,0:T(8,128)S(1)}, f32[1,80,256]{2,1,0:T(8,128)}, u32[]{:S(2)}) copy-start(f32[1,80,256]{2,1,0:T(8,128)} %param.14) | copy-start | bytes 245764
  114.8 21.6 %copy-start.2 = (f32[80]{0:T(128)S(1)}, f32[80]{0:T(128)}, u32[]{:S(2)}) copy-start(f32[80]{0:T(128)} %param.15) | copy-start | bytes 964
  117.8 35.4 %collective-permute-start = (bf16[320,1280]{1,0:T(8,128)(2,1)S(1)}, bf16[320,1280]{1,0:T(8,128)(2,1)S(1)}, u32[]{:S(2)}, u32[]{:S(2)}) collective-permute-start(bf16[320,1280]{1,0:T(8,128)(2,1)S(1)} %get-tuple-element.28), channel_id=1, source_target_pairs={{0,1},{1,2},{2,3},{3,0},{4,5},{5,6},{6,7},{7,4},{8,9},{9,10},{10,1... | collective-permute-start | bytes 2457608 | tf_op jit(solution)/shard_map/ppermute | solution.py:757
  117.8 53.9 %collective-permute-start.1 = (bf16[320,1280]{1,0:T(8,128)(2,1)S(1)}, bf16[320,1280]{1,0:T(8,128)(2,1)}, u32[]{:S(2)}, u32[]{:S(2)}) collective-permute-start(bf16[320,1280]{1,0:T(8,128)(2,1)S(1)} %get-tuple-element.27), channel_id=1, source_target_pairs={{0,2},{1,3},{2,0},{3,1},{4,6},{5,7},{6,4},{7,5},{8,10},{9,11},{10,... | collective-permute-start | bytes 2457608 | tf_op jit(solution)/shard_map/ppermute | solution.py:757
  136.2 35.5 %collective-permute-start.2 = (bf16[320,1280]{1,0:T(8,128)(2,1)S(1)}, bf16[320,1280]{1,0:T(8,128)(2,1)}, u32[]{:S(2)}, u32[]{:S(2)}) collective-permute-start(bf16[320,1280]{1,0:T(8,128)(2,1)S(1)} %get-tuple-element.26), channel_id=1, source_target_pairs={{0,3},{1,0},{2,1},{3,2},{4,7},{5,4},{6,5},{7,6},{8,11},{9,8},{10,9... | collective-permute-start | bytes 2457608 | tf_op jit(solution)/shard_map/ppermute | solution.py:757
  153.2 19.1 %copy-start = (bf16[320,1280]{1,0:T(8,128)(2,1)}, bf16[320,1280]{1,0:T(8,128)(2,1)S(1)}, u32[]{:S(2)}) copy-start(bf16[320,1280]{1,0:T(8,128)(2,1)S(1)} %collective-permute-done.t1_ref) | copy-start | bytes 2457604

commit v3 on v0

v3 whole, which is shorter than its diff:
```python
import functools
import math

import jax
import jax.numpy as jnp
from jax import lax
from jax.experimental import pallas as pl
from jax.experimental.pallas import tpu as pltpu
from jax.sharding import PartitionSpec as P

NORM_EPS = 1e-05
CLIP_EPS = 1e-06
MESH = pl.DeviceIdType.MESH
F32 = jnp.float32
BF16 = jnp.bfloat16
HIGHEST = lax.Precision.HIGHEST

TOK = 256
HALF = 128
STATE = 128
HEADS = 80
GROUP = 10
LANES = 640
GROUPS = 8
INNER = 5120
MODEL = 1280
CAP = 80.0
SIDE = 4
CTX = 16
RING = 8
OWN = INNER // CTX
WIDE = 384
COLS = MODEL // 16
THIN = 32
EARLY = 3
VMEM_BYTES = 60 * 1024 * 1024


def dot(a, b):
    return jnp.dot(a, b, preferred_element_type=F32)


def dot_nt(a, b):
    return lax.dot_general(a, b, (((1,), (1,)), ((), ())), preferred_element_type=F32)


def rows_of(shape):
    return lax.broadcasted_iota(jnp.int32, shape, 0)


def lanes_of(shape):
    return lax.broadcasted_iota(jnp.int32, shape, 1)


def low_half():
    return lanes_of((TOK, HALF)) < HALF // 2


def pair_cols(columns, pair):
    return jnp.where(low_half(), columns[:, 2 * pair : 2 * pair + 1], columns[:, 2 * pair + 1 : 2 * pair + 2])


def split_pair(values):
    zero = jnp.zeros_like(values)
    return jnp.where(low_half(), values, zero), jnp.where(low_half(), zero, values)


def silu(gate):
    return gate / (1.0 + jnp.exp(-gate))


def lane_block(at, width):
    return pl.ds(pl.multiple_of(at * width, HALF), width)


def layer_kernel(
    scale,
    x_ref,
    z_ref,
    st_ref,
    lr_ref,
    s_ref,
    b_ref,
    c_ref,
    gain_ref,
    w_ref,
    og_ref,
    out_ref,
    grad_ref,
    steps,
    rates,
    cums,
    shifts,
    xbuf,
    sbuf,
    mixed,
    gated,
    coup,
    upper,
    acc,
    rms,
    turned,
    wpad,
    thin,
    full,
    gx,
    ox,
    partial,
    landing,
    relay,
    ybuf,
    term,
    square_own,
    squares,
    chunks,
    paired,
    zsend,
    zrecv,
    fac,
    facs,
    expanded,
    ct,
    pushed,
    arrived,
    running,
    back,
    landed,
    prelay,
    brelay,
    x_sem,
    s_sem,
    out_sem,
    w_send,
    w_recv,
    ring_send,
    ring_recv,
    wy_send,
    wy_recv,
    sib_send,
    sib_recv,
    o_send,
    o_recv,
    g_send,
    g_recv,
    y_send,
    y_recv,
    r_send,
    r_recv,
    yf_send,
    yf_recv,
    q_send,
    q_recv,
    pair_send,
    pair_recv,
    z_send,
    z_recv,
    f_send,
    f_recv,
    p_send,
    p_recv,
    b_send,
    b_recv,
    pr_recv,
    po_send,
    br_recv,
    bo_send,
):
    dp, me = lax.axis_index("dp"), lax.axis_index("ctx")
    core, z = lax.rem(dp, 2), lax.div(dp, 2)
    x, y = lax.div(me, SIDE), lax.rem(me, SIDE)
    partner = dp + 1 - 2 * core

    def remote(src, dst, send, recv, to):
        return pltpu.make_async_remote_copy(
            src_ref=src, dst_ref=dst, send_sem=send, recv_sem=recv, device_id=to, device_id_type=MESH
        )

    def others(body):
        def turn(s, carry):
            body(lax.rem(me + s, CTX))
            return carry

        lax.fori_loop(1, CTX, turn, 0)

    def z_others(body):
        def turn(s, carry):
            body(lax.rem(z + s, RING))
            return carry

        lax.fori_loop(1, RING, turn, 0)

    def load_group(at):
        slot = lax.rem(at, 2)
        return (
            pltpu.make_async_copy(x_ref.at[:, lane_block(at, LANES)], xbuf.at[slot], x_sem.at[slot]),
            pltpu.make_async_copy(s_ref.at[lane_block(at, LANES)], sbuf.at[slot], s_sem.at[slot]),
        )

    def store_group(at):
        slot = lax.rem(at, 2)
        return pltpu.make_async_copy(xbuf.at[slot], out_ref.at[:, lane_block(at, LANES)], out_sem.at[slot])

    for copy in load_group(0):
        copy.start()

    barrier = pltpu.get_barrier_semaphore()

    def greet(to):
        pl.semaphore_signal(barrier, inc=1, device_id=(dp, to), device_id_type=MESH)

    def greet_z(to):
        pl.semaphore_signal(barrier, inc=1, device_id=(2 * to + core, me), device_id_type=MESH)

    others(greet)
    z_others(greet_z)
    pl.semaphore_signal(barrier, inc=1, device_id=(partner, me), device_id_type=MESH)

    wide_w = jnp.concatenate([w_ref[...].astype(F32), jnp.zeros((THIN - OWN // CTX, MODEL), F32)], axis=0)
    wpad[...] = wide_w.astype(BF16)
    odd = lax.rem(y, 2)
    part_of = lax.div(me, RING)

    def thin_from(i):
        return remote(wpad, thin.at[i], w_send.at[i], w_recv.at[i], (dp, RING * odd + i))

    def thin_out(i):
        return SIDE * lax.div(i, 2) + 2 * lax.rem(i, 2) + part_of

    def thin_send(i):
        to = thin_out(i)
        return remote(wpad, thin.at[lax.rem(me, RING)], w_send.at[i], w_recv.at[lax.rem(me, RING)], (dp, to))

    def each_thin_out(body):
        def turn(i, carry):
            @pl.when(thin_out(i) != me)
            def _():
                body(i)

            return carry

        lax.fori_loop(0, RING, turn, 0)

    def block_part(at, which, part):
        row = pl.multiple_of(which * OWN + part * COLS, 16)
        return full.at[at, pl.ds(row, COLS)]

    def ring_copy(way, turn, half, at):
        slot = (way * 4 + turn) * 2 + half
        to = 2 * lax.rem(z + (1 if way == 0 else RING - 1), RING) + core
        block = block_part(at, core, 2 * odd + half)
        return remote(block, block, ring_send.at[slot], ring_recv.at[slot], (to, me))

    def side_copy(at, half, parity):
        to = (dp, x * SIDE + lax.rem(y + (1 if half == 0 else SIDE - 1), SIDE))
        block = block_part(at, core, 2 * parity + half)
        return remote(block, block, wy_send.at[at, half], wy_recv.at[at, half], to)

    def sib_copy(at, which, part):
        block = block_part(at, which, part)
        return remote(block, block, sib_send.at[at, part], sib_recv.at[at, part], (partner, me))

    def x_peer(s):
        return (dp, lax.rem(x + s, SIDE) * SIDE + y)

    def y_peer(s):
        return (dp, x * SIDE + lax.rem(y + s, SIDE))

    def o_copy(s, slot):
        return remote(og_ref, ox.at[slot], o_send.at[s], o_recv.at[s], x_peer(s))

    def o_relay(half, slot):
        block = ox.at[slot, pl.ds(half * HALF, HALF)]
        return remote(block, block, o_send.at[2 * half], o_recv.at[2 * half], x_peer(1 if half == 0 else 3))

    def turned_rows(s, half, count):
        to = lax.rem(x + s, SIDE)
        return turned.at[pl.ds(pl.multiple_of(to * MODEL + half * (MODEL // 2), HALF), count)]

    def g_copy(s, slot):
        return remote(turned_rows(s, 0, MODEL), gx.at[slot], g_send.at[s], g_recv.at[s], x_peer(s))

    def g_far(half):
        to = x_peer(1 if half == 0 else 3)
        return remote(turned_rows(2, half, MODEL // 2), relay.at[half], r_send.at[half], r_recv.at[half], to)

    def g_relay(half, slot):
        block = gx.at[slot, pl.ds(half * (MODEL // 2), MODEL // 2)]
        return remote(relay.at[half], block, g_send.at[2 * half], g_recv.at[2 * half], x_peer(1 if half == 0 else 3))

    def y_far(half):
        block = partial.at[2, pl.ds(half * (OWN // 2), OWN // 2)]
        return remote(block, ybuf.at[half], yf_send.at[half], yf_recv.at[half], y_peer(1 if half == 0 else 3))

    def y_near(side, half):
        rows = pl.ds(half * (OWN // 2), OWN // 2)
        s, slot = 1 + 2 * side, 2 * side + half
        return remote(partial.at[s, rows], landing.at[side, rows], y_send.at[slot], y_recv.at[slot], y_peer(s))

    def square_copy(to, slot):
        return remote(square_own, squares.at[slot], q_send.at[to], q_recv.at[slot], (dp, to))

    pair_copy = remote(chunks.at[1 - core], paired, pair_send, pair_recv, (partner, me))

    def z_copy(to, slot):
        return remote(zsend.at[to], zrecv.at[slot], z_send.at[to], z_recv.at[slot], (2 * to + core, me))

    def piece(ref, owner):
        row = pl.multiple_of(lax.div(owner, SIDE) * THIN, THIN)
        return ref.at[pl.ds(row, THIN), lane_block(lax.rem(owner, SIDE), MODEL)]

    def fac_copy(to, slot):
        return remote(fac, facs.at[slot], f_send.at[to], f_recv.at[slot], (dp, to))

    def push_copy(src, to, slot):
        return remote(piece(pushed, src), arrived.at[slot], p_send.at[to], p_recv.at[slot], (dp, to))

    def back_copy(to, owner):
        return remote(back.at[to], piece(landed, owner), b_send.at[to], b_recv.at[owner], (dp, to))


    for at in range(GROUPS):
        steps[at, :GROUP, :] = st_ref[at * GROUP : (at + 1) * GROUP, :]
    rate_rows = jnp.broadcast_to(jnp.exp(lr_ref[...]), (HALF, HEADS)).T
    for at in range(GROUPS):
        rates[at, :GROUP, :] = rate_rows[at * GROUP : (at + 1) * GROUP, :]
    square = (TOK, TOK)
    coup[...] = jnp.where(rows_of(square) >= lanes_of(square), dot_nt(c_ref[...], b_ref[...]), 0.0)
    upper[...] = jnp.where(rows_of(square) <= lanes_of(square), 1.0, 0.0).astype(F32)
    ct[...] = c_ref[...].astype(F32).T.astype(BF16)
    acc[...] = jnp.zeros_like(acc)
    fac[...] = jnp.zeros_like(fac)

    def forward(at, carry):
        slot = lax.rem(at, 2)

        @pl.when(at + 1 < GROUPS)
        def _():
            for copy in load_group(at + 1):
                copy.start()

        step = steps[at, :GROUP, :]
        drop = -(rates[at, :GROUP, :1] * step)
        cumulative = jnp.dot(drop, upper[...], preferred_element_type=F32, precision=HIGHEST)
        shifted = cumulative - jnp.log(step)
        cums[at, :GROUP, :] = cumulative
        shifts[at, :GROUP, :] = shifted
        columns = cumulative.T
        fac[pl.ds(at, 1), :GROUP] = jnp.exp(columns[TOK - 1 :, :])
        for copy in load_group(at):
            copy.wait()
        for pair in range(GROUP // 2):
            here = slice(pair * HALF, (pair + 1) * HALF)
            parts = split_pair(xbuf[slot, :, here])
            top = bottom = None
            for which in range(2):
                head = 2 * pair + which
                col = columns[:, head : head + 1]
                row = shifted[head : head + 1, :]
                m_top = jnp.exp(jnp.minimum(col[:HALF] - row[:, :HALF], CAP)) * coup[:HALF, :HALF]
                m_bot = jnp.exp(jnp.minimum(col[HALF:] - row, CAP)) * coup[HALF:, :]
                t = dot(m_top.astype(BF16), parts[which][:HALF])
                b = dot(m_bot.astype(BF16), parts[which])
                top = t if top is None else top + t
                bottom = b if bottom is None else bottom + b
            inside = jnp.concatenate([top, bottom], axis=0)
            carried = dot_nt(c_ref[...], sbuf[slot, here, :])
            value = inside + carried * jnp.exp(pair_cols(columns, pair))
            lanes = pl.ds(pl.multiple_of(at * LANES + pair * HALF, HALF), HALF)
            mix = value * silu(z_ref[:, lanes].astype(F32))
            mixed[at, :, here] = mix
            acc[...] += mix * mix
        return carry

    def arriving(turn, half):
        for way in (0, 1):
            if turn < 3 or half == way:
                yield way, lax.rem(z + (RING - turn - 1 if way == 0 else turn + 1), RING)

    def arrive(turn, half):
        for way, at in arriving(turn, half):
            ring_copy(way, turn, half, at).wait_recv()
            if turn < 2 or (turn == 2 and half == way):
                ring_copy(way, turn + 1, half, at).start()
            side_copy(at, half, odd).start()
            sib_copy(at, core, 2 * odd + half).start()

    def arrive_side(turn, half):
        for _, at in arriving(turn, half):
            side_copy(at, half, 1 - odd).wait_recv()
            sib_copy(at, core, 2 * (1 - odd) + half).start()

    lax.fori_loop(0, EARLY, forward, 0)
    pl.semaphore_wait(barrier, CTX - 1 + RING - 1 + 1)
    def far_route(to):
        tx, ty = lax.div(to, SIDE), lax.rem(to, SIDE)
        dx, dy = lax.rem(tx - x + SIDE, SIDE), lax.rem(ty - y + SIDE, SIDE)
        over_y = jnp.logical_and(dy == 2, lax.rem(dx, 2) == 1)
        over_x = jnp.logical_and(dx == 2, lax.rem(dy, 2) == 1)
        via = jnp.where(over_y, tx * SIDE + lax.rem(y + 3, SIDE), lax.rem(x + 3, SIDE) * SIDE + ty)
        slot = jnp.where(over_y, lax.div(dx, 2), 2 + lax.div(dy, 2))
        return jnp.logical_or(over_y, over_x), via, slot

    def hand_on(slot):
        source_x, source_y = ((3, 1), (1, 1), (1, 3), (1, 1))[slot]
        source = lax.rem(x + source_x, SIDE) * SIDE + lax.rem(y + source_y, SIDE)
        target = x * SIDE + lax.rem(y + 3, SIDE) if slot < 2 else lax.rem(x + 3, SIDE) * SIDE + y
        return source, target

    def push_far(to, via, slot):
        return remote(piece(pushed, to), prelay.at[slot], p_send.at[to], pr_recv.at[slot], (dp, via))

    def push_on(slot):
        source, target = hand_on(slot)
        return remote(prelay.at[slot], arrived.at[source], po_send.at[slot], p_recv.at[source], (dp, target))

    def push_far_wait(slot):
        return remote(prelay.at[slot], prelay.at[slot], po_send.at[slot], pr_recv.at[slot], (dp, hand_on(slot)[0]))

    def back_far(to, via, slot):
        return remote(back.at[to], brelay.at[slot], b_send.at[to], br_recv.at[slot], (dp, via))

    def back_on(slot):
        source, target = hand_on(slot)
        return remote(brelay.at[slot], piece(landed, source), bo_send.at[slot], b_recv.at[source], (dp, target))

    def back_far_wait(slot):
        return remote(brelay.at[slot], brelay.at[slot], bo_send.at[slot], br_recv.at[slot], (dp, hand_on(slot)[0]))

    def send_either(to, near_copy, far_copy):
        far, via, slot = far_route(to)

        @pl.when(jnp.logical_and(to != me, jnp.logical_not(far)))
        def _():
            near_copy(to).start()

        @pl.when(far)
        def _():
            far_copy(to, via, slot).start()

    each_thin_out(lambda i: thin_send(i).start())
    for s in (1, 3):
        o_copy(s, x).start()
    lax.fori_loop(EARLY, GROUPS, forward, 0)

    r = lax.rsqrt(jnp.sum(acc[...], axis=1, keepdims=True) * (1.0 / INNER) + NORM_EPS)
    rms[...] = jnp.broadcast_to(r, rms.shape)

    def finish_norm(at, carry):
        lanes = lane_block(at, LANES)
        normed = mixed[at] * rms[:, :1] * gain_ref[:, lanes]
        gated[at] = normed.astype(BF16)
        turned[lanes, :] = normed.T.astype(BF16)
        return carry

    lax.fori_loop(0, GROUPS, finish_norm, 0)

    for half in range(2):
        g_far(half).start()
    for s in (1, 3):
        g_copy(s, x).start()

    def wait_thin(i, carry):
        k = RING * odd + i

        @pl.when(k != me)
        def _():
            thin_from(i).wait_recv()

        return carry

    @pl.when(part_of == odd)
    def _():
        thin[lax.rem(me, RING)] = wpad[...]

    lax.fori_loop(0, RING, wait_thin, 0)
    rows = [thin[k][: OWN // CTX].astype(F32) for k in range(RING)]
    half_rows = pl.ds(pl.multiple_of(core * OWN + odd * (OWN // 2), 16), OWN // 2)
    full[z, half_rows] = jnp.concatenate(rows, axis=0).astype(BF16)
    for half in range(2):
        for way in range(2):
            ring_copy(way, 0, half, z).start()
        side_copy(z, half, odd).start()
        sib_copy(z, core, 2 * odd + half).start()

    left, right = lax.rem(x + 3, SIDE), lax.rem(x + 1, SIDE)
    gx[x] = turned[pl.ds(pl.multiple_of(x * MODEL, MODEL), MODEL), :]
    ox[x] = og_ref[...]
    others(lambda to: fac_copy(to, me).start())
    acc[...] = jnp.zeros_like(acc)

    def product(at):
        for part in range(SIDE):
            sib_copy(at, 1 - core, part).wait_recv()
        value = dot_nt(og_ref[...], full[at])
        mixed[at] = value
        both = value * gated[at].astype(F32)
        total = acc[...]
        for i in range(LANES // HALF):
            total += both[:, i * HALF : (i + 1) * HALF]
        acc[...] = total

    def weight_part(s):
        rows = pl.ds(pl.multiple_of(lax.rem(y + s, SIDE) * OWN, OWN), OWN)
        total = None
        for source in range(SIDE):
            part = dot(gx[source, rows, :], ox[source])
            total = part if total is None else total + part
        partial[s] = total.astype(BF16)

    def near(step):
        return lax.rem(z + step, RING)

    arrive(0, 0)
    arrive(0, 1)
    o_copy(1, left).wait_recv()
    o_relay(0, left).start()
    o_copy(3, right).wait_recv()
    o_relay(1, right).start()
    for half in range(2):
        side_copy(z, half, 1 - odd).wait_recv()
        sib_copy(z, core, 2 * (1 - odd) + half).start()
    arrive(1, 0)
    arrive_side(0, 0)
    product(z)
    arrive(1, 1)
    arrive_side(0, 1)
    for half in range(2):
        g_far(half).wait_recv()
        g_relay(half, left if half == 0 else right).start()
    arrive(2, 0)
    arrive_side(1, 0)
    product(near(1))
    product(near(7))
    arrive(2, 1)
    arrive_side(1, 1)
    arrive(3, 0)
    arrive_side(2, 0)
    product(near(2))
    product(near(6))
    arrive(3, 1)
    arrive_side(2, 1)
    arrive_side(3, 0)
    product(near(3))
    product(near(5))
    arrive_side(3, 1)
    product(near(4))
    mean = jnp.sum(acc[...], axis=1, keepdims=True) * (1.0 / INNER)
    acc[...] = jnp.broadcast_to(mean, acc.shape)

    def norm_back(at, carry):
        columns = cums[at].T
        for pair in range(GROUP // 2):
            here = slice(pair * HALF, (pair + 1) * HALF)
            lanes = pl.ds(pl.multiple_of(at * LANES + pair * HALF, HALF), HALF)
            gain = gain_ref[:, lanes]
            inner = gain * mixed[at, :, here] - gated[at, :, here].astype(F32) * (1.0 / gain) * acc[...]
            yg = silu(z_ref[:, lanes].astype(F32)) * rms[...] * inner
            gated[at, :, here] = yg.astype(BF16)
            weighted = (yg * jnp.exp(pair_cols(columns, pair))).astype(BF16)
            pushed[:, lanes] = dot(ct[...], weighted).astype(BF16)
        return carry

    for i in range(SIDE):
        quarter = lax.rem(y + 2 + i, SIDE)
        lax.fori_loop(2 * quarter, 2 * quarter + 2, norm_back, 0)

        def send_quarter(row, carry):
            send_either(SIDE * row + quarter, lambda to: push_copy(to, to, me), push_far)
            return carry

        lax.fori_loop(0, SIDE, send_quarter, 0)

    far = lax.rem(x + 2, SIDE)
    for half in range(2):
        o_relay(half, far).wait_recv()
        g_relay(half, far).wait_recv()
    g_copy(1, left).wait_recv()
    g_copy(3, right).wait_recv()
    weight_part(2)
    for half in range(2):
        y_far(half).start()
    weight_part(1)
    y_near(0, 1).start()
    weight_part(3)
    y_near(1, 0).start()
    weight_part(0)

    coup[...] = jnp.where(rows_of(square) <= lanes_of(square), dot_nt(b_ref[...], c_ref[...]), 0.0)

    def inside_back(at, carry):
        shifted = shifts[at]
        columns = shifted.T
        for pair in range(GROUP // 2):
            here = slice(pair * HALF, (pair + 1) * HALF)
            parts = split_pair(gated[at, :, here])
            top = bottom = None
            for which in range(2):
                head = 2 * pair + which
                col = columns[:, head : head + 1]
                row = cums[at, head : head + 1, :]
                m_top = jnp.exp(jnp.minimum(row - col[:HALF], CAP)) * coup[:HALF, :]
                m_bot = jnp.exp(jnp.minimum(row[:, HALF:] - col[HALF:], CAP)) * coup[HALF:, HALF:]
                t = dot(m_top.astype(BF16), parts[which])
                b = dot(m_bot.astype(BF16), parts[which][HALF:])
                top = t if top is None else top + t
                bottom = b if bottom is None else bottom + b
            mixed[at, :HALF, here] = top
            mixed[at, HALF:, here] = bottom
        return carry

    for slot in range(SIDE):
        push_far_wait(slot).wait_recv()
        push_on(slot).start()
    lax.fori_loop(0, 4, inside_back, 0)
    for half in range(2):
        y_far(half).wait_recv()
        at = slice(half * (OWN // 2), (half + 1) * (OWN // 2))
        added = partial[1 + 2 * half, at].astype(F32) + ybuf[half].astype(F32)
        partial[1 + 2 * half, at] = added.astype(BF16)
        y_near(half, half).start()
    lax.fori_loop(4, GROUPS, inside_back, 0)

    arrived[me] = piece(pushed, me)[...]
    facs[me] = fac[...]
    others(lambda k: fac_copy(k, k).wait_recv())
    shape = (HALF, LANES)
    hot = jnp.where(rows_of(shape) == lax.shift_right_logical(lanes_of(shape), 6), 1.0, 0.0).astype(F32)
    listed = jnp.concatenate([facs[k] for k in range(CTX)], axis=0)
    expanded[...] = jnp.dot(listed, hot, preferred_element_type=F32, precision=HIGHEST)
    running[...] = jnp.zeros_like(running)

    def chain(turn, carry):
        k = CTX - 1 - turn

        @pl.when(k != me)
        def _():
            push_copy(k, k, k).wait_recv()

        now = running[...]
        back[k] = now.astype(BF16)

        first = k * GROUPS + 2 * lax.rem(me, SIDE)
        factor = jnp.concatenate([expanded[pl.ds(first, 1), :], expanded[pl.ds(first + 1, 1), :]], axis=1)
        running[...] = factor * now + arrived[k].astype(F32)
        return carry

    lax.fori_loop(0, CTX, chain, 0)
    piece(landed, me)[...] = back[me]
    for side in range(2):
        for half in range(2):
            y_near(side, half).wait_recv()
    total = partial[0].astype(F32)
    for side in range(2):
        total += landing[side].astype(F32)
    term[:OWN, :] = total
    term[OWN:, :] = jnp.zeros((WIDE - OWN, MODEL), F32)
    folded = jnp.sum((total * total).reshape(OWN // 8, 8, MODEL), axis=0)
    part = folded[:, :HALF]
    for i in range(1, MODEL // HALF):
        part += folded[:, i * HALF : (i + 1) * HALF]
    square_own[...] = part
    others(lambda to: square_copy(to, me).start())

    def send_back(to, carry):
        send_either(to, lambda k: back_copy(k, me), back_far)
        return carry

    lax.fori_loop(0, CTX, send_back, 0)
    others(lambda k: square_copy(k, k).wait_recv())
    squares[me] = square_own[...]
    all_squares = squares[0]
    for k in range(1, CTX):
        all_squares += squares[k]
    whole = jnp.sum(jnp.sum(all_squares, axis=1, keepdims=True), axis=0, keepdims=True)
    clip = jnp.minimum(1.0, lax.rsqrt(whole + CLIP_EPS)) * scale
    for i in range(MODEL // HALF):
        block = (term[:, i * HALF : (i + 1) * HALF] * clip).T
        lo = i * HALF
        while lo < (i + 1) * HALF:
            owner = lo // COLS
            hi = min((i + 1) * HALF, (owner + 1) * COLS)
            at = slice(lo - owner * COLS, hi - owner * COLS)
            chunks[owner % 2, owner // 2, at] = block[lo - i * HALF : hi - i * HALF].astype(BF16)
            lo = hi
    pair_copy.start()

    def combine(at, carry):
        slot = lax.rem(at, 2)

        @pl.when(at >= 2)
        def _():
            store_group(at - 2).wait()

        last = (cums[at][:, TOK - 1 :] - shifts[at]).T
        ended = dot(b_ref[...], landed[:, lane_block(at, LANES)])
        for pair in range(GROUP // 2):
            here = slice(pair * HALF, (pair + 1) * HALF)
            value = mixed[at, :, here] + ended[:, here] * jnp.exp(pair_cols(last, pair))
            xbuf[slot, :, here] = value.astype(BF16)
        store_group(at).start()
        return carry

    for slot in range(SIDE):
        back_far_wait(slot).wait_recv()
        back_on(slot).start()
    pair_copy.wait_recv()

    def add_pair(i, carry):
        zsend[i] = (chunks[core, i].astype(F32) + paired[i].astype(F32)).astype(BF16)
        return carry

    lax.fori_loop(0, RING, add_pair, 0)
    z_others(lambda to: z_copy(to, z).start())
    others(lambda k: back_copy(me, k).wait_recv())
    lax.fori_loop(0, GROUPS, combine, 0)
    z_others(lambda k: z_copy(k, k).wait_recv())
    zrecv[z] = zsend[z]
    summed = zrecv[0].astype(F32)
    for k in range(1, RING):
        summed += zrecv[k].astype(F32)
    grad_ref[...] = summed[:, :OWN]

    store_group(GROUPS - 2).wait()
    store_group(GROUPS - 1).wait()

    def finish(to):
        fac_copy(to, me).wait_send()
        push_copy(to, to, me).wait_send()
        square_copy(to, me).wait_send()
        back_copy(to, me).wait_send()

    others(finish)
    pair_copy.wait_send()
    z_others(lambda to: z_copy(to, z).wait_send())
    each_thin_out(lambda i: thin_send(i).wait_send())
    for s in (1, 3):
        o_copy(s, x).wait_send()
        g_copy(s, x).wait_send()
    for half in range(2):
        o_relay(half, left if half == 0 else right).wait_send()
        g_far(half).wait_send()
        g_relay(half, left if half == 0 else right).wait_send()
        y_far(half).wait_send()
        for side in range(2):
            y_near(side, half).wait_send()
    for turn in range(4):
        for half in range(2):
            for way in range(2):
                if turn == 3 and half != way:
                    continue
                at = lax.rem(z + (RING - turn if way == 0 else turn), RING)
                ring_copy(way, turn, half, at).wait_send()

    for slot in range(SIDE):
        push_on(slot).wait_send()
        back_on(slot).wait_send()

    def finish_sib(at, carry):
        for part in range(SIDE):
            sib_copy(at, core, part).wait_send()
        return carry

    lax.fori_loop(0, RING, finish_sib, 0)

    def finish_side(at):
        for half in range(2):
            side_copy(at, half, odd).wait_send()

    z_others(finish_side)
    finish_side(z)


def layer(scale, *operands):
    vmem = pl.BlockSpec(memory_space=pltpu.VMEM)
    hbm = pl.BlockSpec(memory_space=pl.ANY)
    dma = pltpu.SemaphoreType.DMA
    ram = pltpu.VMEM
    return pl.pallas_call(
        functools.partial(layer_kernel, scale),
        out_shape=(jax.ShapeDtypeStruct((TOK, INNER), BF16), jax.ShapeDtypeStruct((COLS, OWN), F32)),
        in_specs=[hbm, vmem, vmem, vmem, hbm] + [vmem] * 5,
        out_specs=(hbm, vmem),
        scratch_shapes=[
            ram((GROUPS, 16, TOK), F32),
            ram((GROUPS, 16, HALF), F32),
            ram((GROUPS, 16, TOK), F32),
            ram((GROUPS, 16, TOK), F32),
            ram((2, TOK, LANES), BF16),
            ram((2, LANES, STATE), BF16),
            ram((GROUPS, TOK, LANES), F32),
            ram((GROUPS, TOK, LANES), BF16),
            ram((TOK, TOK), F32),
            ram((TOK, TOK), F32),
            ram((TOK, HALF), F32),
            ram((TOK, HALF), F32),
            ram((INNER, TOK), BF16),
            ram((THIN, MODEL), BF16),
            ram((RING, THIN, MODEL), BF16),
            ram((RING, 2 * OWN, MODEL), BF16),
            ram((SIDE, MODEL, TOK), BF16),
            ram((SIDE, TOK, MODEL), BF16),
            ram((SIDE, OWN, MODEL), BF16),
            ram((2, OWN, MODEL), BF16),
            ram((2, MODEL // 2, TOK), BF16),
            ram((2, OWN // 2, MODEL), BF16),
            ram((WIDE, MODEL), F32),
            ram((8, HALF), F32),
            ram((CTX, 8, HALF), F32),
            ram((2, RING, COLS, WIDE), BF16),
            ram((RING, COLS, WIDE), BF16),
            ram((RING, COLS, WIDE), BF16),
            ram((RING, COLS, WIDE), BF16),
            ram((8, HALF), F32),
            ram((CTX, 8, HALF), F32),
            ram((HALF, LANES), F32),
            ram((STATE, TOK), BF16),
            ram((STATE, INNER), BF16),
            ram((CTX, THIN, MODEL), BF16),
            ram((THIN, MODEL), F32),
            ram((CTX, THIN, MODEL), BF16),
            ram((STATE, INNER), BF16),
            ram((SIDE, THIN, MODEL), BF16),
            ram((SIDE, THIN, MODEL), BF16),
        ]
        + [dma((2,))] * 3
        + [dma((RING,))] * 2
        + [dma((16,))] * 2
        + [dma((RING, 2))] * 2
        + [dma((RING, SIDE))] * 2
        + [dma((SIDE,))] * 6
        + [dma((2,))] * 4
        + [dma((CTX,))] * 2
        + [dma, dma]
        + [dma((RING,))] * 2
        + [dma((CTX,))] * 6
        + [dma((SIDE,))] * 4,
        compiler_params=pltpu.CompilerParams(
            collective_id=0, has_side_effects=True, vmem_limit_bytes=VMEM_BYTES
        ),
        cost_estimate=pl.CostEstimate(flops=14 * 10**9, bytes_accessed=100 * 10**6, transcendentals=3 * 10**7),
        name="layer",
    )(*operands)


def per_device(
    ssm_input,
    gate_input,
    input_map,
    output_map,
    step_size,
    log_rate,
    entry_state,
    norm_gain,
    out_weight,
    out_grad,
):
    scale = math.sqrt(INNER * MODEL / lax.axis_size("dp"))
    input_grad, summed = layer(
        scale,
        ssm_input[0],
        gate_input[0],
        step_size[0],
        log_rate.reshape(1, HEADS),
        entry_state.reshape(INNER, STATE),
        input_map[0],
        output_map[0],
        norm_gain.reshape(1, INNER),
        out_weight,
        out_grad[0],
    )
    return (input_grad[None], summed.T)


def solution(mesh):
    placed = (
        P("dp", "ctx", None),
        P("dp", "ctx", None),
        P("dp", "ctx", None),
        P("dp", "ctx", None),
        P("dp", None, "ctx"),
        P(),
        P("dp", "ctx", None, None, None),
        P(),
        P(("dp", "ctx"), None),
        P("dp", "ctx", None),
    )
    return jax.shard_map(
        per_device,
        mesh=mesh,
        in_specs=placed,
        out_specs=(P("dp", "ctx", None), P("ctx", "dp")),
        check_vma=False,
    )
```

time: 710 us -> 157 us (0.22)
  the two profiles are of different devices: /device:TPU:7 before, /device:TPU:24 now
where the time goes in v3:
time: 157 us
  Pallas kernels  152 us (97%)
  local copies, waits for them, and re-layouts  4.09 us (3%)
    pallas_call x1, Pallas kernels, layer(): pl.pallas_call(functools.partial(layer_kernel, scale), out_shape=(jax.Sha...  152 us
    unnamed x4, local copies, waits for them, and re-layouts  4.09 us

profile of v3, /device:TPU:24, one launch (start us, length us, event | category | flops | bytes accessed | tf_op | source)
XLA Modules:
  0.0 156.9 jit_solution(14467990638102792420)
XLA Ops:
  0.6 152.1 %layer.1 = (bf16[256,5120]{1,0:T(8,128)(2,1)}, f32[80,320]{1,0:T(8,128)}) custom-call(bf16[256,5120]{1,0:T(8,128)(2,1)} %bitcast.13, bf16[256,5120]{1,0:T(8,128)(2,1)} %bitcast.14, f32[80,256]{1,0:T(8,128)} %bitcast.17, f32[1,80]{1,0:T(1,128)} %bitcast.21, bf16[5120,128]{1,0:T(8,128)(2,1)} %bitcast.15, bf16[256,128]{1,0:T(8,128)(2,1)} %bitcast.18, ...), custom_call_target="tpu_custom_call" | custom-call | flops 14000000000 | bytes 100000000 | tf_op jit(solution)/shard_map/layer/pallas_call | solution.py:778
  152.8 0.0 copy-start
  152.8 3.4 %copy.14 = bf16[1,256,5120]{2,1,0:T(8,128)(2,1)} copy(bf16[1,256,5120]{2,1,0:T(8,128)(2,1)} %bitcast.11) | data formatting | bytes 5242880
  156.2 0.0 copy-done
  156.2 0.6 copy.15
Async XLA Ops:
  152.8 3.4 %copy-start = (f32[80,320]{1,0:T(8,128)S(1)}, f32[80,320]{1,0:T(8,128)}, u32[]{:S(2)}) copy-start(f32[80,320]{1,0:T(8,128)} %get-tuple-element.5) | copy-start | bytes 307204

commit v4 on v3

--- a/solution.py
+++ b/solution.py
@@ -33,6 +33,7 @@
 COLS = MODEL // 16
 THIN = 32
 EARLY = 3
+THINAT = 6
 VMEM_BYTES = 60 * 1024 * 1024
 
 
@@ -76,7 +77,7 @@
 def layer_kernel(
     scale,
     x_ref,
-    z_ref,
+    z_hbm,
     st_ref,
     lr_ref,
     s_ref,
@@ -93,6 +94,7 @@
     shifts,
     xbuf,
     sbuf,
+    z_ref,
     mixed,
     gated,
     coup,
@@ -125,8 +127,7 @@
     running,
     back,
     landed,
-    prelay,
-    brelay,
+    gate_sem,
     x_sem,
     s_sem,
     out_sem,
@@ -160,15 +161,25 @@
     p_recv,
     b_send,
     b_recv,
-    pr_recv,
-    po_send,
-    br_recv,
-    bo_send,
 ):
     dp, me = lax.axis_index("dp"), lax.axis_index("ctx")
     core, z = lax.rem(dp, 2), lax.div(dp, 2)
     x, y = lax.div(me, SIDE), lax.rem(me, SIDE)
     partner = dp + 1 - 2 * core
+    first = core == 0
+    a, r = jnp.where(first, x, y), jnp.where(first, y, x)
+
+    def over_x(s):
+        return lax.rem(x + s, SIDE) * SIDE + y
+
+    def over_y(s):
+        return x * SIDE + lax.rem(y + s, SIDE)
+
+    def a_peer(s):
+        return (dp, jnp.where(first, over_x(s), over_y(s)))
+
+    def r_peer(s):
+        return (dp, jnp.where(first, over_y(s), over_x(s)))
 
     def remote(src, dst, send, recv, to):
         return pltpu.make_async_remote_copy(
@@ -196,12 +207,17 @@
             pltpu.make_async_copy(s_ref.at[lane_block(at, LANES)], sbuf.at[slot], s_sem.at[slot]),
         )
 
-    def store_group(at):
-        slot = lax.rem(at, 2)
+    def store_group(at, slot):
         return pltpu.make_async_copy(xbuf.at[slot], out_ref.at[:, lane_block(at, LANES)], out_sem.at[slot])
+
+    def load_gate(at):
+        lanes = lane_block(at, LANES)
+        return pltpu.make_async_copy(z_hbm.at[:, lanes], z_ref.at[:, lanes], gate_sem.at[at])
 
     for copy in load_group(0):
         copy.start()
+    for at in range(GROUPS):
+        load_gate(at).start()
 
     barrier = pltpu.get_barrier_semaphore()
 
@@ -215,16 +231,21 @@
     z_others(greet_z)
     pl.semaphore_signal(barrier, inc=1, device_id=(partner, me), device_id_type=MESH)
 
-    wide_w = jnp.concatenate([w_ref[...].astype(F32), jnp.zeros((THIN - OWN // CTX, MODEL), F32)], axis=0)
-    wpad[...] = wide_w.astype(BF16)
-    odd = lax.rem(y, 2)
+    weights = w_ref[...].astype(F32)
+    wpad[:, :MODEL] = weights[:16].astype(BF16)
+    rest = [weights[16:, WIDE * i : min(WIDE * (i + 1), MODEL)] for i in range(SIDE)]
+    rest[-1] = jnp.concatenate([rest[-1], jnp.zeros((4, WIDE - rest[-1].shape[1]), F32)], axis=1)
+    wpad[:, MODEL:] = jnp.concatenate(rest, axis=0).astype(BF16)
+
+    odd = lax.rem(r, 2)
     part_of = lax.div(me, RING)
 
     def thin_from(i):
         return remote(wpad, thin.at[i], w_send.at[i], w_recv.at[i], (dp, RING * odd + i))
 
     def thin_out(i):
-        return SIDE * lax.div(i, 2) + 2 * lax.rem(i, 2) + part_of
+        along, across = 2 * lax.rem(i, 2) + part_of, lax.div(i, 2)
+        return jnp.where(first, SIDE * across + along, SIDE * along + across)
 
     def thin_send(i):
         to = thin_out(i)
@@ -251,50 +272,44 @@
         return remote(block, block, ring_send.at[slot], ring_recv.at[slot], (to, me))
 
     def side_copy(at, half, parity):
-        to = (dp, x * SIDE + lax.rem(y + (1 if half == 0 else SIDE - 1), SIDE))
         block = block_part(at, core, 2 * parity + half)
+        to = r_peer(1 if half == 0 else 3)
         return remote(block, block, wy_send.at[at, half], wy_recv.at[at, half], to)
 
     def sib_copy(at, which, part):
         block = block_part(at, which, part)
         return remote(block, block, sib_send.at[at, part], sib_recv.at[at, part], (partner, me))
 
-    def x_peer(s):
-        return (dp, lax.rem(x + s, SIDE) * SIDE + y)
-
-    def y_peer(s):
-        return (dp, x * SIDE + lax.rem(y + s, SIDE))
-
     def o_copy(s, slot):
-        return remote(og_ref, ox.at[slot], o_send.at[s], o_recv.at[s], x_peer(s))
+        return remote(og_ref, ox.at[slot], o_send.at[s], o_recv.at[s], a_peer(s))
 
     def o_relay(half, slot):
         block = ox.at[slot, pl.ds(half * HALF, HALF)]
-        return remote(block, block, o_send.at[2 * half], o_recv.at[2 * half], x_peer(1 if half == 0 else 3))
+        return remote(block, block, o_send.at[2 * half], o_recv.at[2 * half], a_peer(1 if half == 0 else 3))
 
     def turned_rows(s, half, count):
-        to = lax.rem(x + s, SIDE)
+        to = lax.rem(a + s, SIDE)
         return turned.at[pl.ds(pl.multiple_of(to * MODEL + half * (MODEL // 2), HALF), count)]
 
     def g_copy(s, slot):
-        return remote(turned_rows(s, 0, MODEL), gx.at[slot], g_send.at[s], g_recv.at[s], x_peer(s))
+        return remote(turned_rows(s, 0, MODEL), gx.at[slot], g_send.at[s], g_recv.at[s], a_peer(s))
 
     def g_far(half):
-        to = x_peer(1 if half == 0 else 3)
+        to = a_peer(1 if half == 0 else 3)
         return remote(turned_rows(2, half, MODEL // 2), relay.at[half], r_send.at[half], r_recv.at[half], to)
 
     def g_relay(half, slot):
         block = gx.at[slot, pl.ds(half * (MODEL // 2), MODEL // 2)]
-        return remote(relay.at[half], block, g_send.at[2 * half], g_recv.at[2 * half], x_peer(1 if half == 0 else 3))
+        return remote(relay.at[half], block, g_send.at[2 * half], g_recv.at[2 * half], a_peer(1 if half == 0 else 3))
 
     def y_far(half):
         block = partial.at[2, pl.ds(half * (OWN // 2), OWN // 2)]
-        return remote(block, ybuf.at[half], yf_send.at[half], yf_recv.at[half], y_peer(1 if half == 0 else 3))
+        return remote(block, ybuf.at[half], yf_send.at[half], yf_recv.at[half], r_peer(1 if half == 0 else 3))
 
     def y_near(side, half):
         rows = pl.ds(half * (OWN // 2), OWN // 2)
         s, slot = 1 + 2 * side, 2 * side + half
-        return remote(partial.at[s, rows], landing.at[side, rows], y_send.at[slot], y_recv.at[slot], y_peer(s))
+        return remote(partial.at[s, rows], landing.at[side, rows], y_send.at[slot], y_recv.at[slot], r_peer(s))
 
     def square_copy(to, slot):
         return remote(square_own, squares.at[slot], q_send.at[to], q_recv.at[slot], (dp, to))
@@ -348,6 +363,7 @@
         fac[pl.ds(at, 1), :GROUP] = jnp.exp(columns[TOK - 1 :, :])
         for copy in load_group(at):
             copy.wait()
+        load_gate(at).wait()
         for pair in range(GROUP // 2):
             here = slice(pair * HALF, (pair + 1) * HALF)
             parts = split_pair(xbuf[slot, :, here])
@@ -391,73 +407,13 @@
 
     lax.fori_loop(0, EARLY, forward, 0)
     pl.semaphore_wait(barrier, CTX - 1 + RING - 1 + 1)
-    def far_route(to):
-        tx, ty = lax.div(to, SIDE), lax.rem(to, SIDE)
-        dx, dy = lax.rem(tx - x + SIDE, SIDE), lax.rem(ty - y + SIDE, SIDE)
-        over_y = jnp.logical_and(dy == 2, lax.rem(dx, 2) == 1)
-        over_x = jnp.logical_and(dx == 2, lax.rem(dy, 2) == 1)
-        via = jnp.where(over_y, tx * SIDE + lax.rem(y + 3, SIDE), lax.rem(x + 3, SIDE) * SIDE + ty)
-        slot = jnp.where(over_y, lax.div(dx, 2), 2 + lax.div(dy, 2))
-        return jnp.logical_or(over_y, over_x), via, slot
-
-    def hand_on(slot):
-        source_x, source_y = ((3, 1), (1, 1), (1, 3), (1, 1))[slot]
-        source = lax.rem(x + source_x, SIDE) * SIDE + lax.rem(y + source_y, SIDE)
-        target = x * SIDE + lax.rem(y + 3, SIDE) if slot < 2 else lax.rem(x + 3, SIDE) * SIDE + y
-        return source, target
-
-    def push_far(to, via, slot):
-        return remote(piece(pushed, to), prelay.at[slot], p_send.at[to], pr_recv.at[slot], (dp, via))
-
-    def push_on(slot):
-        source, target = hand_on(slot)
-        return remote(prelay.at[slot], arrived.at[source], po_send.at[slot], p_recv.at[source], (dp, target))
-
-    def push_far_wait(slot):
-        return remote(prelay.at[slot], prelay.at[slot], po_send.at[slot], pr_recv.at[slot], (dp, hand_on(slot)[0]))
-
-    def back_far(to, via, slot):
-        return remote(back.at[to], brelay.at[slot], b_send.at[to], br_recv.at[slot], (dp, via))
-
-    def back_on(slot):
-        source, target = hand_on(slot)
-        return remote(brelay.at[slot], piece(landed, source), bo_send.at[slot], b_recv.at[source], (dp, target))
-
-    def back_far_wait(slot):
-        return remote(brelay.at[slot], brelay.at[slot], bo_send.at[slot], br_recv.at[slot], (dp, hand_on(slot)[0]))
-
-    def send_either(to, near_copy, far_copy):
-        far, via, slot = far_route(to)
-
-        @pl.when(jnp.logical_and(to != me, jnp.logical_not(far)))
+    def push_to(to):
+        @pl.when(to != me)
         def _():
-            near_copy(to).start()
-
-        @pl.when(far)
-        def _():
-            far_copy(to, via, slot).start()
+            push_copy(to, to, me).start()
 
     each_thin_out(lambda i: thin_send(i).start())
-    for s in (1, 3):
-        o_copy(s, x).start()
-    lax.fori_loop(EARLY, GROUPS, forward, 0)
-
-    r = lax.rsqrt(jnp.sum(acc[...], axis=1, keepdims=True) * (1.0 / INNER) + NORM_EPS)
-    rms[...] = jnp.broadcast_to(r, rms.shape)
-
-    def finish_norm(at, carry):
-        lanes = lane_block(at, LANES)
-        normed = mixed[at] * rms[:, :1] * gain_ref[:, lanes]
-        gated[at] = normed.astype(BF16)
-        turned[lanes, :] = normed.T.astype(BF16)
-        return carry
-
-    lax.fori_loop(0, GROUPS, finish_norm, 0)
-
-    for half in range(2):
-        g_far(half).start()
-    for s in (1, 3):
-        g_copy(s, x).start()
+    lax.fori_loop(EARLY, THINAT, forward, 0)
 
     def wait_thin(i, carry):
         k = RING * odd + i
@@ -473,7 +429,11 @@
         thin[lax.rem(me, RING)] = wpad[...]
 
     lax.fori_loop(0, RING, wait_thin, 0)
-    rows = [thin[k][: OWN // CTX].astype(F32) for k in range(RING)]
+    rows = []
+    for k in range(RING):
+        value = thin[k].astype(F32)
+        rest = [value[4 * i : 4 * i + 4, MODEL:] for i in range(SIDE)]
+        rows += [value[:, :MODEL], jnp.concatenate(rest, axis=1)[:, :MODEL]]
     half_rows = pl.ds(pl.multiple_of(core * OWN + odd * (OWN // 2), 16), OWN // 2)
     full[z, half_rows] = jnp.concatenate(rows, axis=0).astype(BF16)
     for half in range(2):
@@ -481,10 +441,34 @@
             ring_copy(way, 0, half, z).start()
         side_copy(z, half, odd).start()
         sib_copy(z, core, 2 * odd + half).start()
-
-    left, right = lax.rem(x + 3, SIDE), lax.rem(x + 1, SIDE)
-    gx[x] = turned[pl.ds(pl.multiple_of(x * MODEL, MODEL), MODEL), :]
-    ox[x] = og_ref[...]
+    for s in (1, 3):
+        o_copy(s, a).start()
+    lax.fori_loop(THINAT, GROUPS, forward, 0)
+
+    inverse = lax.rsqrt(jnp.sum(acc[...], axis=1, keepdims=True) * (1.0 / INNER) + NORM_EPS)
+    rms[...] = jnp.broadcast_to(inverse, rms.shape)
+
+    def finish_norm(at, carry):
+        lanes = lane_block(at, LANES)
+        normed = mixed[at] * rms[:, :1] * gain_ref[:, lanes]
+        gated[at] = normed.astype(BF16)
+        rows = normed.T.astype(BF16)
+        for which in range(2):
+            block = 2 * at + which
+            place = jnp.where(first, block, SIDE * lax.rem(block, SIDE) + lax.div(block, SIDE))
+            turned[pl.ds(pl.multiple_of(place * OWN, OWN), OWN), :] = rows[which * OWN : (which + 1) * OWN]
+        return carry
+
+    lax.fori_loop(0, GROUPS, finish_norm, 0)
+
+    for half in range(2):
+        g_far(half).start()
+    for s in (1, 3):
+        g_copy(s, a).start()
+
+    left, right = lax.rem(a + 3, SIDE), lax.rem(a + 1, SIDE)
+    gx[a] = turned[pl.ds(pl.multiple_of(a * MODEL, MODEL), MODEL), :]
+    ox[a] = og_ref[...]
     others(lambda to: fac_copy(to, me).start())
     acc[...] = jnp.zeros_like(acc)
 
@@ -500,7 +484,7 @@
         acc[...] = total
 
     def weight_part(s):
-        rows = pl.ds(pl.multiple_of(lax.rem(y + s, SIDE) * OWN, OWN), OWN)
+        rows = pl.ds(pl.multiple_of(lax.rem(r + s, SIDE) * OWN, OWN), OWN)
         total = None
         for source in range(SIDE):
             part = dot(gx[source, rows, :], ox[source])
@@ -542,8 +526,28 @@
     arrive_side(3, 0)
     product(near(3))
     product(near(5))
+    far = lax.rem(a + 2, SIDE)
+    for half in range(2):
+        o_relay(half, far).wait_recv()
+        g_relay(half, far).wait_recv()
+    g_copy(1, left).wait_recv()
+    g_copy(3, right).wait_recv()
+    weight_part(2)
+    for half in range(2):
+        y_far(half).start()
+    weight_part(1)
+    y_near(0, 1).start()
+    weight_part(3)
+    y_near(1, 0).start()
     arrive_side(3, 1)
     product(near(4))
+    weight_part(0)
+    for half in range(2):
+        y_far(half).wait_recv()
+        at = slice(half * (OWN // 2), (half + 1) * (OWN // 2))
+        added = partial[1 + 2 * half, at].astype(F32) + ybuf[half].astype(F32)
+        partial[1 + 2 * half, at] = added.astype(BF16)
+        y_near(half, half).start()
     mean = jnp.sum(acc[...], axis=1, keepdims=True) * (1.0 / INNER)
     acc[...] = jnp.broadcast_to(mean, acc.shape)
 
@@ -560,30 +564,11 @@
             pushed[:, lanes] = dot(ct[...], weighted).astype(BF16)
         return carry
 
-    for i in range(SIDE):
-        quarter = lax.rem(y + 2 + i, SIDE)
+    for shift in (2, 1, 3, 0):
+        quarter = lax.rem(y + shift, SIDE)
         lax.fori_loop(2 * quarter, 2 * quarter + 2, norm_back, 0)
-
-        def send_quarter(row, carry):
-            send_either(SIDE * row + quarter, lambda to: push_copy(to, to, me), push_far)
-            return carry
-
-        lax.fori_loop(0, SIDE, send_quarter, 0)
-
-    far = lax.rem(x + 2, SIDE)
-    for half in range(2):
-        o_relay(half, far).wait_recv()
-        g_relay(half, far).wait_recv()
-    g_copy(1, left).wait_recv()
-    g_copy(3, right).wait_recv()
-    weight_part(2)
-    for half in range(2):
-        y_far(half).start()
-    weight_part(1)
-    y_near(0, 1).start()
-    weight_part(3)
-    y_near(1, 0).start()
-    weight_part(0)
+        for row in range(SIDE):
+            push_to(SIDE * lax.rem(x + (2, 1, 3, 0)[row], SIDE) + quarter)
 
     coup[...] = jnp.where(rows_of(square) <= lanes_of(square), dot_nt(b_ref[...], c_ref[...]), 0.0)
 
@@ -608,44 +593,8 @@
             mixed[at, HALF:, here] = bottom
         return carry
 
-    for slot in range(SIDE):
-        push_far_wait(slot).wait_recv()
-        push_on(slot).start()
     lax.fori_loop(0, 4, inside_back, 0)
-    for half in range(2):
-        y_far(half).wait_recv()
-        at = slice(half * (OWN // 2), (half + 1) * (OWN // 2))
-        added = partial[1 + 2 * half, at].astype(F32) + ybuf[half].astype(F32)
-        partial[1 + 2 * half, at] = added.astype(BF16)
-        y_near(half, half).start()
     lax.fori_loop(4, GROUPS, inside_back, 0)
-
-    arrived[me] = piece(pushed, me)[...]
-    facs[me] = fac[...]
-    others(lambda k: fac_copy(k, k).wait_recv())
-    shape = (HALF, LANES)
-    hot = jnp.where(rows_of(shape) == lax.shift_right_logical(lanes_of(shape), 6), 1.0, 0.0).astype(F32)
-    listed = jnp.concatenate([facs[k] for k in range(CTX)], axis=0)
-    expanded[...] = jnp.dot(listed, hot, preferred_element_type=F32, precision=HIGHEST)
-    running[...] = jnp.zeros_like(running)
-
-    def chain(turn, carry):
-        k = CTX - 1 - turn
-
-        @pl.when(k != me)
-        def _():
-            push_copy(k, k, k).wait_recv()
-
-        now = running[...]
-        back[k] = now.astype(BF16)
-
-        first = k * GROUPS + 2 * lax.rem(me, SIDE)
-        factor = jnp.concatenate([expanded[pl.ds(first, 1), :], expanded[pl.ds(first + 1, 1), :]], axis=1)
-        running[...] = factor * now + arrived[k].astype(F32)
-        return carry
-
-    lax.fori_loop(0, CTX, chain, 0)
-    piece(landed, me)[...] = back[me]
     for side in range(2):
         for half in range(2):
             y_near(side, half).wait_recv()
@@ -661,11 +610,36 @@
     square_own[...] = part
     others(lambda to: square_copy(to, me).start())
 
-    def send_back(to, carry):
-        send_either(to, lambda k: back_copy(k, me), back_far)
+    arrived[me] = piece(pushed, me)[...]
+    facs[me] = fac[...]
+    others(lambda k: fac_copy(k, k).wait_recv())
+    shape = (HALF, LANES)
+    hot = jnp.where(rows_of(shape) == lax.shift_right_logical(lanes_of(shape), 6), 1.0, 0.0).astype(F32)
+    listed = jnp.concatenate([facs[k] for k in range(CTX)], axis=0)
+    expanded[...] = jnp.dot(listed, hot, preferred_element_type=F32, precision=HIGHEST)
+    running[...] = jnp.zeros_like(running)
+
+    def chain(turn, carry):
+        k = CTX - 1 - turn
+
+        @pl.when(k != me)
+        def _():
+            push_copy(k, k, k).wait_recv()
+
+        now = running[...]
+        back[k] = now.astype(BF16)
+
+        @pl.when(k != me)
+        def _():
+            back_copy(k, me).start()
+
+        first = k * GROUPS + 2 * lax.rem(me, SIDE)
+        factor = jnp.concatenate([expanded[pl.ds(first, 1), :], expanded[pl.ds(first + 1, 1), :]], axis=1)
+        running[...] = factor * now + arrived[k].astype(F32)
         return carry
 
-    lax.fori_loop(0, CTX, send_back, 0)
+    lax.fori_loop(0, CTX, chain, 0)
+    piece(landed, me)[...] = back[me]
     others(lambda k: square_copy(k, k).wait_recv())
     squares[me] = square_own[...]
     all_squares = squares[0]
@@ -684,25 +658,18 @@
             lo = hi
     pair_copy.start()
 
-    def combine(at, carry):
-        slot = lax.rem(at, 2)
-
-        @pl.when(at >= 2)
-        def _():
-            store_group(at - 2).wait()
-
+    def combine(at, count):
+        slot = count % 2
+        if count >= 2:
+            store_group(at, slot).wait()
         last = (cums[at][:, TOK - 1 :] - shifts[at]).T
         ended = dot(b_ref[...], landed[:, lane_block(at, LANES)])
         for pair in range(GROUP // 2):
             here = slice(pair * HALF, (pair + 1) * HALF)
             value = mixed[at, :, here] + ended[:, here] * jnp.exp(pair_cols(last, pair))
             xbuf[slot, :, here] = value.astype(BF16)
-        store_group(at).start()
-        return carry
-
-    for slot in range(SIDE):
-        back_far_wait(slot).wait_recv()
-        back_on(slot).start()
+        store_group(at, slot).start()
+
     pair_copy.wait_recv()
 
     def add_pair(i, carry):
@@ -711,8 +678,21 @@
 
     lax.fori_loop(0, RING, add_pair, 0)
     z_others(lambda to: z_copy(to, z).start())
-    others(lambda k: back_copy(me, k).wait_recv())
-    lax.fori_loop(0, GROUPS, combine, 0)
+    for turn, shift in enumerate((0, 1, 3, 2)):
+        quarter = lax.rem(y + shift, SIDE)
+
+        def wait_back(row, carry):
+            k = SIDE * row + quarter
+
+            @pl.when(k != me)
+            def _():
+                back_copy(me, k).wait_recv()
+
+            return carry
+
+        lax.fori_loop(0, SIDE, wait_back, 0)
+        for i in range(2):
+            combine(2 * quarter + i, 2 * turn + i)
     z_others(lambda k: z_copy(k, k).wait_recv())
     zrecv[z] = zsend[z]
     summed = zrecv[0].astype(F32)
@@ -720,8 +700,8 @@
         summed += zrecv[k].astype(F32)
     grad_ref[...] = summed[:, :OWN]
 
-    store_group(GROUPS - 2).wait()
-    store_group(GROUPS - 1).wait()
+    store_group(0, 0).wait()
+    store_group(0, 1).wait()
 
     def finish(to):
         fac_copy(to, me).wait_send()
@@ -734,8 +714,8 @@
     z_others(lambda to: z_copy(to, z).wait_send())
     each_thin_out(lambda i: thin_send(i).wait_send())
     for s in (1, 3):
-        o_copy(s, x).wait_send()
-        g_copy(s, x).wait_send()
+        o_copy(s, a).wait_send()
+        g_copy(s, a).wait_send()
     for half in range(2):
         o_relay(half, left if half == 0 else right).wait_send()
         g_far(half).wait_send()
@@ -751,10 +731,6 @@
                 at = lax.rem(z + (RING - turn if way == 0 else turn), RING)
                 ring_copy(way, turn, half, at).wait_send()
 
-    for slot in range(SIDE):
-        push_on(slot).wait_send()
-        back_on(slot).wait_send()
-
     def finish_sib(at, carry):
         for part in range(SIDE):
             sib_copy(at, core, part).wait_send()
@@ -778,7 +754,7 @@
     return pl.pallas_call(
         functools.partial(layer_kernel, scale),
         out_shape=(jax.ShapeDtypeStruct((TOK, INNER), BF16), jax.ShapeDtypeStruct((COLS, OWN), F32)),
-        in_specs=[hbm, vmem, vmem, vmem, hbm] + [vmem] * 5,
+        in_specs=[hbm, hbm, vmem, vmem, hbm] + [vmem] * 5,
         out_specs=(hbm, vmem),
         scratch_shapes=[
             ram((GROUPS, 16, TOK), F32),
@@ -787,6 +763,7 @@
             ram((GROUPS, 16, TOK), F32),
             ram((2, TOK, LANES), BF16),
             ram((2, LANES, STATE), BF16),
+            ram((TOK, INNER), BF16),
             ram((GROUPS, TOK, LANES), F32),
             ram((GROUPS, TOK, LANES), BF16),
             ram((TOK, TOK), F32),
@@ -794,8 +771,8 @@
             ram((TOK, HALF), F32),
             ram((TOK, HALF), F32),
             ram((INNER, TOK), BF16),
-            ram((THIN, MODEL), BF16),
-            ram((RING, THIN, MODEL), BF16),
+            ram((16, MODEL + WIDE), BF16),
+            ram((RING, 16, MODEL + WIDE), BF16),
             ram((RING, 2 * OWN, MODEL), BF16),
             ram((SIDE, MODEL, TOK), BF16),
             ram((SIDE, TOK, MODEL), BF16),
@@ -819,9 +796,8 @@
             ram((THIN, MODEL), F32),
             ram((CTX, THIN, MODEL), BF16),
             ram((STATE, INNER), BF16),
-            ram((SIDE, THIN, MODEL), BF16),
-            ram((SIDE, THIN, MODEL), BF16),
         ]
+        + [dma((GROUPS,))]
         + [dma((2,))] * 3
         + [dma((RING,))] * 2
         + [dma((16,))] * 2
@@ -832,8 +808,7 @@
         + [dma((CTX,))] * 2
         + [dma, dma]
         + [dma((RING,))] * 2
-        + [dma((CTX,))] * 6
-        + [dma((SIDE,))] * 4,
+        + [dma((CTX,))] * 6,
         compiler_params=pltpu.CompilerParams(
             collective_id=0, has_side_effects=True, vmem_limit_bytes=VMEM_BYTES
         ),

time: 157 us -> 139 us (0.89)
  the two profiles are of different devices: /device:TPU:24 before, /device:TPU:7 now
where the time goes in v4:
time: 139 us
  Pallas kernels  134 us (96%)
  local copies, waits for them, and re-layouts  4.09 us (3%)
    pallas_call x1, Pallas kernels, layer(): pl.pallas_call(functools.partial(layer_kernel, scale), out_shape=(jax.Sha...  134 us
    unnamed x4, local copies, waits for them, and re-layouts  4.09 us

profile of v4, /device:TPU:7, one launch (start us, length us, event | category | flops | bytes accessed | tf_op | source)
XLA Modules:
  0.0 138.5 jit_solution(11256144720156808283)
XLA Ops:
  0.6 133.8 %layer.1 = (bf16[256,5120]{1,0:T(8,128)(2,1)}, f32[80,320]{1,0:T(8,128)}) custom-call(bf16[256,5120]{1,0:T(8,128)(2,1)} %bitcast.13, bf16[256,5120]{1,0:T(8,128)(2,1)} %bitcast.14, f32[80,256]{1,0:T(8,128)} %bitcast.17, f32[1,80]{1,0:T(1,128)} %bitcast.21, bf16[5120,128]{1,0:T(8,128)(2,1)} %bitcast.15, bf16[256,128]{1,0:T(8,128)(2,1)} %bitcast.18, ...), custom_call_target="tpu_custom_call" | custom-call | flops 14000000000 | bytes 100000000 | tf_op jit(solution)/shard_map/layer/pallas_call | solution.py:754
  134.4 0.0 copy-start
  134.4 3.4 %copy.14 = bf16[1,256,5120]{2,1,0:T(8,128)(2,1)} copy(bf16[1,256,5120]{2,1,0:T(8,128)(2,1)} %bitcast.11) | data formatting | bytes 5242880
  137.9 0.0 copy-done
  137.9 0.6 copy.15
Async XLA Ops:
  134.4 3.4 %copy-start = (f32[80,320]{1,0:T(8,128)S(1)}, f32[80,320]{1,0:T(8,128)}, u32[]{:S(2)}) copy-start(f32[80,320]{1,0:T(8,128)} %get-tuple-element.5) | copy-start | bytes 307204

commit v5 on v4

--- a/solution.py
+++ b/solution.py
@@ -526,6 +526,7 @@
     arrive_side(3, 0)
     product(near(3))
     product(near(5))
+    arrive_side(3, 1)
     far = lax.rem(a + 2, SIDE)
     for half in range(2):
         o_relay(half, far).wait_recv()
@@ -539,7 +540,6 @@
     y_near(0, 1).start()
     weight_part(3)
     y_near(1, 0).start()
-    arrive_side(3, 1)
     product(near(4))
     weight_part(0)
     for half in range(2):
@@ -629,10 +629,6 @@
         now = running[...]
         back[k] = now.astype(BF16)
 
-        @pl.when(k != me)
-        def _():
-            back_copy(k, me).start()
-
         first = k * GROUPS + 2 * lax.rem(me, SIDE)
         factor = jnp.concatenate([expanded[pl.ds(first, 1), :], expanded[pl.ds(first + 1, 1), :]], axis=1)
         running[...] = factor * now + arrived[k].astype(F32)
@@ -640,6 +636,7 @@
 
     lax.fori_loop(0, CTX, chain, 0)
     piece(landed, me)[...] = back[me]
+    others(lambda to: back_copy(to, me).start())
     others(lambda k: square_copy(k, k).wait_recv())
     squares[me] = square_own[...]
     all_squares = squares[0]

time: 139 us -> 134 us (0.964); the launches traced: 139 us -> 132 us
  Pallas kernels: 134 us -> 127 us
    pallas_call x1, Pallas kernels: 134 us -> 127 us  [layer(): pl.pallas_call(functools.partial(layer_kernel, scale), out_shape=(jax.Sha...]
where the time goes in v5:
time: 134 us; the launch traced here: 132 us
  Pallas kernels  127 us (95%)
  local copies, waits for them, and re-layouts  4.09 us (3%)
    pallas_call x1, Pallas kernels, layer(): pl.pallas_call(functools.partial(layer_kernel, scale), out_shape=(jax.Sha...  127 us
    unnamed x4, local copies, waits for them, and re-layouts  4.09 us

profile of v5, /device:TPU:7, one launch (start us, length us, event | category | flops | bytes accessed | tf_op | source)
XLA Modules:
  0.0 132.1 jit_solution(137743907138305078)
XLA Ops:
  0.6 127.4 %layer.1 = (bf16[256,5120]{1,0:T(8,128)(2,1)}, f32[80,320]{1,0:T(8,128)}) custom-call(bf16[256,5120]{1,0:T(8,128)(2,1)} %bitcast.13, bf16[256,5120]{1,0:T(8,128)(2,1)} %bitcast.14, f32[80,256]{1,0:T(8,128)} %bitcast.17, f32[1,80]{1,0:T(1,128)} %bitcast.21, bf16[5120,128]{1,0:T(8,128)(2,1)} %bitcast.15, bf16[256,128]{1,0:T(8,128)(2,1)} %bitcast.18, ...), custom_call_target="tpu_custom_call" | custom-call | flops 14000000000 | bytes 100000000 | tf_op jit(solution)/shard_map/layer/pallas_call | solution.py:751
  128.0 0.0 copy-start
  128.0 3.4 %copy.14 = bf16[1,256,5120]{2,1,0:T(8,128)(2,1)} copy(bf16[1,256,5120]{2,1,0:T(8,128)(2,1)} %bitcast.11) | data formatting | bytes 5242880
  131.5 0.0 copy-done
  131.5 0.6 copy.15
Async XLA Ops:
  128.0 3.4 %copy-start = (f32[80,320]{1,0:T(8,128)S(1)}, f32[80,320]{1,0:T(8,128)}, u32[]{:S(2)}) copy-start(f32[80,320]{1,0:T(8,128)} %get-tuple-element.5) | copy-start | bytes 307204

commit v6 on v5

--- a/solution.py
+++ b/solution.py
@@ -33,7 +33,7 @@
 COLS = MODEL // 16
 THIN = 32
 EARLY = 3
-THINAT = 6
+THINAT = 7
 VMEM_BYTES = 60 * 1024 * 1024
 
 

time: 134 us -> 134 us (level)
  no operation moved by 1% of the time
where the time goes in v6:
time: 134 us; the launch traced here: 131 us
  Pallas kernels  127 us (95%)
  local copies, waits for them, and re-layouts  4.09 us (3%)
    pallas_call x1, Pallas kernels, layer(): pl.pallas_call(functools.partial(layer_kernel, scale), out_shape=(jax.Sha...  127 us
    unnamed x4, local copies, waits for them, and re-layouts  4.09 us

profile of v6, /device:TPU:7, one launch (start us, length us, event | category | flops | bytes accessed | tf_op | source)
XLA Modules:
  0.0 131.3 jit_solution(4022275209340767205)
XLA Ops:
  0.6 126.5 %layer.1 = (bf16[256,5120]{1,0:T(8,128)(2,1)}, f32[80,320]{1,0:T(8,128)}) custom-call(bf16[256,5120]{1,0:T(8,128)(2,1)} %bitcast.13, bf16[256,5120]{1,0:T(8,128)(2,1)} %bitcast.14, f32[80,256]{1,0:T(8,128)} %bitcast.17, f32[1,80]{1,0:T(1,128)} %bitcast.21, bf16[5120,128]{1,0:T(8,128)(2,1)} %bitcast.15, bf16[256,128]{1,0:T(8,128)(2,1)} %bitcast.18, ...), custom_call_target="tpu_custom_call" | custom-call | flops 14000000000 | bytes 100000000 | tf_op jit(solution)/shard_map/layer/pallas_call | solution.py:751
  127.2 0.0 copy-start
  127.2 3.4 %copy.14 = bf16[1,256,5120]{2,1,0:T(8,128)(2,1)} copy(bf16[1,256,5120]{2,1,0:T(8,128)(2,1)} %bitcast.11) | data formatting | bytes 5242880
  130.6 0.0 copy-done
  130.6 0.6 copy.15
Async XLA Ops:
  127.2 3.4 %copy-start = (f32[80,320]{1,0:T(8,128)S(1)}, f32[80,320]{1,0:T(8,128)}, u32[]{:S(2)}) copy-start(f32[80,320]{1,0:T(8,128)} %get-tuple-element.5) | copy-start | bytes 307204
